TPU v7x, 1024 devices: a whole 8x8x8 slice. The times are simulated.
1024 devices in a mesh: blk: 32 (over z_hi, y), col: 32 (over x, z_lo, core).
Axes of the slice: x: 8, y: 8, z: 8 (z_hi: 4, z_lo: 2; z = z_hi * 2 + z_lo), core: 2. Of those that a mesh axis runs over, the one named last changes fastest.
Arguments:
- pvals: bfloat16 [256, 4, 128, 128], P('blk'), may hold values from -1 to 1
- pcols: int32 [256, 4], P('blk'), may hold values from 0 to 255, as said below
- out_cols: int32 [256, 32], P('blk', 'col'), may hold values from 0 to 255, as said below
Outputs:
- purified: bfloat16 [256, 32, 128, 128], P('blk', 'col')
Inputs may be any that keep to these rules, and one draw needn't show every extreme that they name: `pcols`: each row r lists 4 distinct block columns, each within 8 of r counted cyclically modulo 256; slot 0 is r itself. `out_cols`: each row r lists 32 distinct block columns, each within 16 of r counted cyclically modulo 256.
All inputs are finite; a program needn't handle non-finite values.
Results may differ from a plain program's by a relative error of at most 0.0049.
Values may be sent and summed in bfloat16 or wider, within the bound.
No kernel may reach another device: no remote copies, remote signals or barrier semaphores. Data moves between devices by JAX's collectives and lax.ppermute only.
A program may use at most 64 MiB of HBM per device.

v0:
```python
import jax
import jax.numpy as jnp
from jax import lax
from jax.sharding import PartitionSpec as P

BAND = 8


def shifted(block, axis, distance):
    devices = range(lax.axis_size(axis))
    route = [((i - distance) % len(devices), i) for i in devices]
    return lax.ppermute(block, axis, route)


def select_blocks(located, targets, window_blocks, window_columns):
    fetched_columns = window_columns[located]
    matches = fetched_columns[None, :, :] == targets[:, None, None]
    found = jnp.any(matches, axis=2)
    position = jnp.argmax(matches.astype(jnp.int32), axis=2)
    picked = window_blocks[located[None, :], position]
    return jnp.where(found[:, :, None, None], picked, jnp.zeros_like(picked))


def square_rows(blocks, columns, wanted, window_blocks, window_columns, window_start, total_rows):

    def square_one_row(inputs):
        row_blocks, row_columns, row_wanted = inputs
        located = jnp.mod(row_columns - window_start, total_rows)
        chosen = select_blocks(located, row_wanted, window_blocks, window_columns)
        product = jnp.einsum(
            "aij,sajk->sik", row_blocks, chosen, preferred_element_type=jnp.float32
        )
        return product.astype(jnp.bfloat16)

    return lax.map(square_one_row, (blocks, columns, wanted))


def cube_rows(
    squared, squared_columns, wanted, window_blocks, window_columns, window_start, total_rows
):

    def cube_one_row(inputs):
        squared_row, row_columns, row_wanted = inputs
        located = jnp.mod(row_columns - window_start, total_rows).astype(jnp.int32)
        chosen = select_blocks(located, row_wanted, window_blocks, window_columns)
        return jnp.einsum("qij,oqjk->oik", squared_row, chosen, preferred_element_type=jnp.float32)

    return lax.map(cube_one_row, (squared, squared_columns, wanted))


def body(pvals, pcols, out_cols):
    row_count = pvals.shape[0]
    total_rows = row_count * lax.axis_size("blk")
    band_half = min(BAND, (total_rows - 1) // 4)
    out_half = min(2 * band_half, (total_rows - 1) // 2)
    reach_owners = (out_half + row_count - 1) // row_count
    window_start = (lax.axis_index("blk") - reach_owners) * row_count
    farthest = shifted((pvals, pcols), "blk", -reach_owners)

    def advance(running, unused):
        moved = shifted((running[0], running[1]), "blk", 1)
        return (moved, moved)

    final_panel, passed = lax.scan(advance, farthest, None, length=2 * reach_owners)
    window_blocks = jnp.concatenate([jnp.flip(passed[0], 0), farthest[0][None]], 0)
    window_columns = jnp.concatenate([jnp.flip(passed[1], 0), farthest[1][None]], 0)
    window_blocks = window_blocks.reshape((-1,) + pvals.shape[1:])
    window_columns = window_columns.reshape((-1, pcols.shape[1]))
    own_squared = square_rows(
        pvals, pcols, out_cols, window_blocks, window_columns, window_start, total_rows
    )
    all_squared, all_columns = (
        lax.all_gather(own_squared, "col", axis=1, tiled=True),
        lax.all_gather(out_cols, "col", axis=1, tiled=True),
    )
    cubed = cube_rows(
        all_squared, all_columns, out_cols, window_blocks, window_columns, window_start, total_rows
    )
    return (3.0 * own_squared.astype(jnp.float32) - 2.0 * cubed).astype(jnp.bfloat16)


def solution(mesh):
    placed = (P("blk", None, None, None), P("blk", None), P("blk", "col"))
    return jax.shard_map(
        body, mesh=mesh, in_specs=placed, out_specs=P("blk", "col", None, None), check_vma=False
    )
```

profile of v0, /device:TPU:1, one launch (start us, length us, event | category | flops | bytes accessed | tf_op | source)
XLA Modules:
  0.0 495.1 jit_solution(311047537864637783)
XLA Ops:
  6.5 21.3 %collective-permute-start.2 = (bf16[8,4,128,128]{3,2,1,0:T(8,128)(2,1)}, bf16[8,4,128,128]{3,2,1,0:T(8,128)(2,1)S(1)}, u32[]{:S(2)}, u32[]{:S(2)}) collective-permute-start(bf16[8,4,128,128]{3,2,1,0:T(8,128)(2,1)} %param.9), channel_id=1, source_target_pairs={{64,0},{96,32},{128,64},{160,96},{192,128},{224,160},{256,192},{28... | collective-permute-start | bytes 3145736 | tf_op jit(solution)/shard_map/ppermute | solution.py:12
  27.9 3.5 collective-permute-start.3
  32.2 45.2 %collective-permute-done.3 = s32[8,4]{0,1:T(4,128)S(1)} collective-permute-done((s32[8,4]{0,1:T(4,128)}, s32[8,4]{0,1:T(4,128)S(1)}, u32[]{:S(2)}, u32[]{:S(2)}) %collective-permute-start.3) | collective-permute-done | bytes 160 | tf_op jit(solution)/shard_map/ppermute | solution.py:12
  77.5 188.3 %while.40 = (s32[]{:T(128)}, bf16[8,4,128,128]{3,2,1,0:T(8,128)(2,1)S(1)}, s32[8,4]{0,1:T(4,128)S(1)}, bf16[4,8,4,128,128]{4,3,2,1,0:T(8,128)(2,1)}, s32[4,8,4]{1,2,0:T(4,128)S(1)}, /*index=5*/s32[]{:T(128)}) while((s32[]{:T(128)}, bf16[8,4,128,128]{3,2,1,0:T(8,128)(2,1)S(1)}, s32[8,4]{0,1:T(4,128)S(1)}, ...), condition=%wide.region_1.2_spmd, body=%wide.region_0.1_spmd.sunk | while | flops 2 | bytes 8393637 | solution.py:64
  77.5 5.0 %collective-permute-start = (bf16[8,4,128,128]{3,2,1,0:T(8,128)(2,1)S(1)}, bf16[8,4,128,128]{3,2,1,0:T(8,128)(2,1)S(1)}, u32[]{:S(2)}, u32[]{:S(2)}) collective-permute-start(bf16[8,4,128,128]{3,2,1,0:T(8,128)(2,1)S(1)} %get-tuple-element.497), channel_id=1, source_target_pairs={{992,0},{0,32},{32,64},{64,96},{96,128},{128,160},{160,192},{192,2... | collective-permute-start | bytes 3145736 | tf_op jit(solution)/shard_map/while/body/eval_jaxpr/ppermute | solution.py:12
  82.5 1.9 collective-permute-start.1
  84.4 48.3 %collective-permute-done.1 = s32[8,4]{0,1:T(4,128)S(1)} collective-permute-done((s32[8,4]{0,1:T(4,128)S(1)}, s32[8,4]{0,1:T(4,128)S(1)}, u32[]{:S(2)}, u32[]{:S(2)}) %collective-permute-start.1) | collective-permute-done | bytes 160 | tf_op jit(solution)/shard_map/while/body/eval_jaxpr/ppermute | solution.py:12
  133.9 1.9 collective-permute-start
  135.8 1.9 collective-permute-start.1
  137.8 40.7 %collective-permute-done.1 = s32[8,4]{0,1:T(4,128)S(1)} collective-permute-done((s32[8,4]{0,1:T(4,128)S(1)}, s32[8,4]{0,1:T(4,128)S(1)}, u32[]{:S(2)}, u32[]{:S(2)}) %collective-permute-start.1) | collective-permute-done | bytes 160 | tf_op jit(solution)/shard_map/while/body/eval_jaxpr/ppermute | solution.py:12
  179.7 1.9 collective-permute-start
  181.6 1.9 collective-permute-start.1
  183.6 36.7 %collective-permute-done.1 = s32[8,4]{0,1:T(4,128)S(1)} collective-permute-done((s32[8,4]{0,1:T(4,128)S(1)}, s32[8,4]{0,1:T(4,128)S(1)}, u32[]{:S(2)}, u32[]{:S(2)}) %collective-permute-start.1) | collective-permute-done | bytes 160 | tf_op jit(solution)/shard_map/while/body/eval_jaxpr/ppermute | solution.py:12
  221.5 1.9 collective-permute-start
  223.4 1.9 collective-permute-start.1
  225.3 39.3 %collective-permute-done.1 = s32[8,4]{0,1:T(4,128)S(1)} collective-permute-done((s32[8,4]{0,1:T(4,128)S(1)}, s32[8,4]{0,1:T(4,128)S(1)}, u32[]{:S(2)}, u32[]{:S(2)}) %collective-permute-start.1) | collective-permute-done | bytes 160 | tf_op jit(solution)/shard_map/while/body/eval_jaxpr/ppermute | solution.py:12
  265.8 4.7 rev.9
  270.7 5.0 %pad_maximum_fusion = bf16[5,8,4,128,128]{4,3,2,1,0:T(8,128)(2,1)} fusion(bf16[1,8,4,128,128]{4,3,2,1,0:T(8,128)(2,1)S(1)} %bitcast.123, bf16[4,8,4,128,128]{4,3,2,1,0:T(8,128)(2,1)} %rev.9), kind=kLoop, calls=%fused_computation.71 | loop fusion | flops 2621440 | bytes 10485760 | tf_op jit(solution)/shard_map/concatenate | solution.py:65
  275.7 62.8 %while.41 = (s32[]{:T(128)}, bf16[8,1,128,128]{3,2,1,0:T(8,128)(2,1)}, s32[8,4]{1,0:T(8,128)S(1)}, s32[]{:T(128)}, s32[40,4]{1,0:T(8,128)S(1)}, /*index=5*/s32[8...) while((s32[]{:T(128)}, bf16[8,1,128,128]{3,2,1,0:T(8,128)(2,1)}, ...), condition=%wide.region_5.6_spmd, body=%wide.region_2.5_spmd.sunk | while | flops 16860448 | bytes 693909 | solution.py:35
  278.6 3.1 gather_fusion.1
  286.4 3.1 gather_fusion.1
  289.5 1.2 fusion.46
  294.2 3.1 gather_fusion.1
  297.3 1.2 fusion.46
  302.1 3.1 gather_fusion.1
  309.9 3.1 gather_fusion.1
  317.8 3.1 gather_fusion.1
  325.6 3.1 gather_fusion.1
  333.5 3.1 gather_fusion.1
  338.5 50.0 %all-gather = s32[32,1,8]{2,1,0:T(1,128)S(1)} all-gather(s32[1,1,8]{2,1,0:T(1,128)S(1)} %bitcast.126), channel_id=1, replica_groups=mesh['blk'=32,'col'=32] {'col'}, dimensions={0}, use_global_device_ids=true | all-gather | bytes 1056 | tf_op jit(solution)/shard_map/all_gather | solution.py:74
  388.6 35.8 %all-gather.3.cloned.1.call-done = bf16[8,32,128,128]{3,2,1,0:T(8,128)(2,1)} async-done(((bf16[8,1,128,128]{3,2,1,0:T(8,128)(2,1)}), bf16[8,32,128,128]{3,2,1,0:T(8,128)(2,1)}) %all-gather.3.cloned.1.call-update) | async-done | bytes 8388624 | tf_op jit(solution)/shard_map/all_gather | solution.py:73
  424.4 63.0 %while.42 = (s32[]{:T(128)}, f32[8,1,128,128]{3,2,1,0:T(8,128)S(1)}, s32[8,32]{1,0:T(8,128)S(1)}, s32[]{:T(128)}, s32[40,4]{1,0:T(8,128)S(1)}, /*index=5*/s32[8,...) while((s32[]{:T(128)}, f32[8,1,128,128]{3,2,1,0:T(8,128)S(1)}, ...), condition=%wide.region_9.10_spmd, body=%wide.region_6.9_spmd.sunk | while | flops 134745344 | bytes 4532033 | solution.py:48
  426.9 3.3 gather_fusion.3
  430.1 2.0 convolution_bitcast_fusion.3
  434.8 3.3 gather_fusion.3
  438.0 2.0 convolution_bitcast_fusion.3
  442.6 3.3 gather_fusion.3
  445.9 2.0 convolution_bitcast_fusion.3
  450.5 3.3 gather_fusion.3
  453.8 2.0 convolution_bitcast_fusion.3
  458.4 3.3 gather_fusion.3
  461.6 2.0 convolution_bitcast_fusion.3
  466.2 3.3 gather_fusion.3
  469.5 2.0 convolution_bitcast_fusion.3
  474.1 3.3 gather_fusion.3
  477.4 2.0 convolution_bitcast_fusion.3
  482.0 3.3 gather_fusion.3
  485.3 2.0 convolution_bitcast_fusion.3
  (229 shorter events, 62.4 us)
Async XLA Ops:
  6.5 417.9 %all-gather.3.cloned.1.call-start = ((), (), s32[]{:S(2)}) async-start(), calls=%async_computation | async-start | bytes 8650752 | tf_op jit(solution)/shard_map/all_gather | solution.py:73
  6.5 70.9 %collective-permute-start.2 = (bf16[8,4,128,128]{3,2,1,0:T(8,128)(2,1)}, bf16[8,4,128,128]{3,2,1,0:T(8,128)(2,1)S(1)}, u32[]{:S(2)}, u32[]{:S(2)}) collective-permute-start(bf16[8,4,128,128]{3,2,1,0:T(8,128)(2,1)} %param.9), channel_id=1, source_target_pairs={{64,0},{96,32},{128,64},{160,96},{192,128},{224,160},{256,192},{28... | collective-permute-start | bytes 3145736 | tf_op jit(solution)/shard_map/ppermute | solution.py:12
  27.9 49.5 %collective-permute-start.3 = (s32[8,4]{0,1:T(4,128)}, s32[8,4]{0,1:T(4,128)S(1)}, u32[]{:S(2)}, u32[]{:S(2)}) collective-permute-start(s32[8,4]{0,1:T(4,128)} %param.10), channel_id=1, source_target_pairs={{64,0},{96,32},{128,64},{160,96},{192,128},{224,160},{256,192},{28... | collective-permute-start | bytes 392 | tf_op jit(solution)/shard_map/ppermute | solution.py:12
  77.5 55.2 %collective-permute-start = (bf16[8,4,128,128]{3,2,1,0:T(8,128)(2,1)S(1)}, bf16[8,4,128,128]{3,2,1,0:T(8,128)(2,1)S(1)}, u32[]{:S(2)}, u32[]{:S(2)}) collective-permute-start(bf16[8,4,128,128]{3,2,1,0:T(8,128)(2,1)S(1)} %get-tuple-element.497), channel_id=1, source_target_pairs={{992,0},{0,32},{32,64},{64,96},{96,128},{128,160},{160,192},{192,2... | collective-permute-start | bytes 3145736 | tf_op jit(solution)/shard_map/while/body/eval_jaxpr/ppermute | solution.py:12
  82.5 50.3 %collective-permute-start.1 = (s32[8,4]{0,1:T(4,128)S(1)}, s32[8,4]{0,1:T(4,128)S(1)}, u32[]{:S(2)}, u32[]{:S(2)}) collective-permute-start(s32[8,4]{0,1:T(4,128)S(1)} %get-tuple-element.498), channel_id=1, source_target_pairs={{992,0},{0,32},{32,64},{64,96},{96,128},{128,160},{160,192},{192,2... | collective-permute-start | bytes 392 | tf_op jit(solution)/shard_map/while/body/eval_jaxpr/ppermute | solution.py:12
  133.9 44.6 %collective-permute-start = (bf16[8,4,128,128]{3,2,1,0:T(8,128)(2,1)S(1)}, bf16[8,4,128,128]{3,2,1,0:T(8,128)(2,1)S(1)}, u32[]{:S(2)}, u32[]{:S(2)}) collective-permute-start(bf16[8,4,128,128]{3,2,1,0:T(8,128)(2,1)S(1)} %get-tuple-element.497), channel_id=1, source_target_pairs={{992,0},{0,32},{32,64},{64,96},{96,128},{128,160},{160,192},{192,2... | collective-permute-start | bytes 3145736 | tf_op jit(solution)/shard_map/while/body/eval_jaxpr/ppermute | solution.py:12
  135.8 42.6 %collective-permute-start.1 = (s32[8,4]{0,1:T(4,128)S(1)}, s32[8,4]{0,1:T(4,128)S(1)}, u32[]{:S(2)}, u32[]{:S(2)}) collective-permute-start(s32[8,4]{0,1:T(4,128)S(1)} %get-tuple-element.498), channel_id=1, source_target_pairs={{992,0},{0,32},{32,64},{64,96},{96,128},{128,160},{160,192},{192,2... | collective-permute-start | bytes 392 | tf_op jit(solution)/shard_map/while/body/eval_jaxpr/ppermute | solution.py:12
  179.7 40.6 %collective-permute-start = (bf16[8,4,128,128]{3,2,1,0:T(8,128)(2,1)S(1)}, bf16[8,4,128,128]{3,2,1,0:T(8,128)(2,1)S(1)}, u32[]{:S(2)}, u32[]{:S(2)}) collective-permute-start(bf16[8,4,128,128]{3,2,1,0:T(8,128)(2,1)S(1)} %get-tuple-element.497), channel_id=1, source_target_pairs={{992,0},{0,32},{32,64},{64,96},{96,128},{128,160},{160,192},{192,2... | collective-permute-start | bytes 3145736 | tf_op jit(solution)/shard_map/while/body/eval_jaxpr/ppermute | solution.py:12
  181.6 38.6 %collective-permute-start.1 = (s32[8,4]{0,1:T(4,128)S(1)}, s32[8,4]{0,1:T(4,128)S(1)}, u32[]{:S(2)}, u32[]{:S(2)}) collective-permute-start(s32[8,4]{0,1:T(4,128)S(1)} %get-tuple-element.498), channel_id=1, source_target_pairs={{992,0},{0,32},{32,64},{64,96},{96,128},{128,160},{160,192},{192,2... | collective-permute-start | bytes 392 | tf_op jit(solution)/shard_map/while/body/eval_jaxpr/ppermute | solution.py:12
  221.5 43.2 %collective-permute-start = (bf16[8,4,128,128]{3,2,1,0:T(8,128)(2,1)S(1)}, bf16[8,4,128,128]{3,2,1,0:T(8,128)(2,1)S(1)}, u32[]{:S(2)}, u32[]{:S(2)}) collective-permute-start(bf16[8,4,128,128]{3,2,1,0:T(8,128)(2,1)S(1)} %get-tuple-element.497), channel_id=1, source_target_pairs={{992,0},{0,32},{32,64},{64,96},{96,128},{128,160},{160,192},{192,2... | collective-permute-start | bytes 3145736 | tf_op jit(solution)/shard_map/while/body/eval_jaxpr/ppermute | solution.py:12
  223.4 41.3 %collective-permute-start.1 = (s32[8,4]{0,1:T(4,128)S(1)}, s32[8,4]{0,1:T(4,128)S(1)}, u32[]{:S(2)}, u32[]{:S(2)}) collective-permute-start(s32[8,4]{0,1:T(4,128)S(1)} %get-tuple-element.498), channel_id=1, source_target_pairs={{992,0},{0,32},{32,64},{64,96},{96,128},{128,160},{160,192},{192,2... | collective-permute-start | bytes 392 | tf_op jit(solution)/shard_map/while/body/eval_jaxpr/ppermute | solution.py:12
  270.7 5.0 %copy-start.1 = (s32[8,1]{0,1:T(1,128)S(1)}, s32[8,1]{0,1:T(1,128)}, u32[]{:S(2)}) copy-start(s32[8,1]{0,1:T(1,128)} %param.11) | copy-start | bytes 100
  424.4 63.0 %copy-start = (bf16[8,1,128,128]{3,2,1,0:T(8,128)(2,1)S(1)}, bf16[8,1,128,128]{3,2,1,0:T(8,128)(2,1)}, u32[]{:S(2)}) copy-start(bf16[8,1,128,128]{3,2,1,0:T(8,128)(2,1)} %get-tuple-element.241) | copy-start | bytes 786436
Sparse Core Ops, SparseCore 0:
  338.7 85.7 all-gather.2
where the time goes:
time: 497 us; the launch traced here: 495 us
  waiting for transfers between devices  246 us (49%)
  local copies, waits for them, and re-layouts  87.6 us (18%)
  blocking collectives  50 us (10%)
  starting transfers between devices  43.2 us (9%)
  other arithmetic  27.9 us (6%)
  matrix products  25.9 us (5%)
  between operations  13.5 us (3%)
    ppermute x10, waiting for transfers between devices, shifted(): return lax.ppermute(block, axis, route)  210 us
    gather x16, local copies, waits for them, and re-layouts, select_blocks(): picked = window_blocks[located[None, :], position]  50.6 us
    all_gather x1, blocking collectives, body(): lax.all_gather(out_cols, 'col', axis=1, tiled=True)  50 us
    ppermute x10, starting transfers between devices, shifted(): return lax.ppermute(block, axis, route)  43.2 us
    all_gather x1, waiting for transfers between devices, body(): lax.all_gather(own_squared, 'col', axis=1, tiled=True)  35.8 us
    dot_general x8, matrix products, cube_one_row(): jnp.einsum('qij,oqjk->oik', squared_row, chosen, preferred_element_type=j...  16.2 us
    reduce_or x16, other arithmetic, select_blocks(): found = jnp.any(matches, axis=2)  11.1 us
    dynamic_slice x16, local copies, waits for them, and re-layouts, square_rows(): return lax.map(square_one_row, (blocks, columns, wanted))  10 us
  transfers between devices with their start and end apart: 11, of which 6 were waited for; matrix products, arithmetic and copies ran while one was open for 0% of the time, Pallas kernels for 0%

commit v1 on v0

v1 whole, which is shorter than its diff:
```python
import jax
import jax.numpy as jnp
from jax import lax
from jax.experimental import pallas as pl
from jax.experimental.pallas import tpu as pltpu
from jax.sharding import PartitionSpec as P

REACH = 2
SHIFTS = (1, -1, 2, -2)


def from_blk(array, distance):
    n = lax.axis_size("blk")
    return lax.ppermute(array, "blk", [((i + distance) % n, i) for i in range(n)])


def from_col(array, source_of):
    n = lax.axis_size("col")
    return lax.ppermute(array, "col", [(source_of(i), i) for i in range(n)])


def purify_kernel(
    layout, bs, slots, sites_ref, cols_ref, wanted_ref, skipped_ref, *refs
):
    pieces, out_ref, window, picks, sems = refs[:-4], refs[-4], refs[-3], refs[-2], refs[-1]
    row_count = out_ref.shape[0]
    nothing = window.shape[0] // bs - 1
    copies = []
    for ref, moves in zip(pieces, layout, strict=True):
        for source, target, site, rows in moves:
            start = pl.multiple_of(target + sites_ref[site], bs)
            copies.append(
                pltpu.make_async_copy(
                    ref.at[pl.ds(source, rows)],
                    window.at[pl.ds(start, rows)],
                    sems.at[len(copies)],
                )
            )
            copies[-1].start()
    window[pl.ds(nothing * bs, bs)] = jnp.zeros((bs, window.shape[1]), window.dtype)

    first = REACH * row_count

    def find_row(r, carry):
        column, skipped = wanted_ref[r], skipped_ref[r]
        for a in range(slots):
            base = cols_ref[(first + r) * slots + a] * slots
            for b in range(slots):
                q = cols_ref[base + b]
                found = jnp.int32(nothing)
                for m in range(slots):
                    found = jnp.where(cols_ref[q * slots + m] == column, q * slots + m, found)
                found = jnp.where(q == skipped, nothing, found)
                picks[r * 32 + a * slots + b] = found
                picks[r * 32 + 16 + a * slots + b] = jnp.where(q == column, base + b, nothing)
        return carry

    lax.fori_loop(0, row_count, find_row, 0)
    for copy in copies:
        copy.wait()

    def block(index):
        return window[pl.ds(pl.multiple_of(index * bs, bs), bs)]

    def stack(indices, axis):
        return jnp.concatenate([block(i) for i in indices], axis=axis)

    for r in range(row_count):
        direct, high, low = [], [], []
        for a in range(slots):
            base = cols_ref[(first + r) * slots + a] * slots
            left = stack([base + b for b in range(slots)], 1)
            right = stack([picks[r * 32 + a * slots + b] for b in range(slots)], 0)
            total = jnp.dot(left, right, preferred_element_type=jnp.float32)
            top = total.astype(jnp.bfloat16)
            high.append(top)
            low.append((total - top.astype(jnp.float32)).astype(jnp.bfloat16))
            one = [block(picks[r * 32 + 16 + a * slots + b]) for b in range(slots)]
            direct.append((one[0] + one[1]) + (one[2] + one[3]))
        left = stack([(first + r) * slots + a for a in range(slots)], 1)
        right = jnp.concatenate(
            [jnp.concatenate(part, 0) for part in (direct, high, low)], 1
        )
        sums = jnp.dot(left, right, preferred_element_type=jnp.float32)
        squared = sums[:, :bs].astype(jnp.bfloat16).astype(jnp.float32)
        cubed = sums[:, bs : 2 * bs] + sums[:, 2 * bs :]
        out_ref[r, 0] = (3.0 * squared - 2.0 * cubed).astype(jnp.bfloat16)


def body(pvals, pcols, out_cols):
    row_count, slots, bs, _ = pvals.shape
    panel = row_count * slots * bs
    quarter, eighth = panel // 4, panel // 8
    total_rows = row_count * lax.axis_size("blk")
    own = lax.axis_index("blk")
    place = lax.axis_index("col")
    window_start = (own - REACH) * row_count

    parity, core = (place // 4) % 2, place % 2
    mine = 2 * parity + core
    flat = pvals.reshape(panel, bs)
    own_cols = pcols.reshape(-1)
    tail = jnp.zeros((16, bs), jnp.bfloat16)
    tail = tail.at[0, : own_cols.shape[0]].set(own_cols.astype(jnp.bfloat16))
    parcel = jnp.concatenate(
        [lax.dynamic_slice_in_dim(flat, mine * quarter, quarter, 0), tail], 0
    )
    arrived = [from_blk(parcel, d) for d in SHIFTS]
    from_left = from_col(
        jnp.concatenate([x[:eighth] for x in arrived], 0), lambda i: (i - 4) % 32
    )
    from_right = from_col(
        jnp.concatenate([x[eighth:quarter] for x in arrived], 0), lambda i: (i + 4) % 32
    )
    other = from_col(jnp.concatenate(arrived, 0), lambda i: i ^ 1)
    other_left = from_col(from_left, lambda i: i ^ 1)
    other_right = from_col(from_right, lambda i: i ^ 1)

    def local(ids):
        return jnp.mod(ids - window_start, total_rows).astype(jnp.int32)

    by_shift = {d: x[quarter, : own_cols.shape[0]] for d, x in zip(SHIFTS, arrived)}
    by_shift[0] = own_cols.astype(jnp.bfloat16)
    window_cols = jnp.concatenate([by_shift[d] for d in range(-REACH, REACH + 1)])
    window_cols = local(window_cols.astype(jnp.int32))
    wanted = local(out_cols[:, 0])
    bound = REACH * row_count
    offsets = jnp.mod(wanted - jnp.arange(row_count), total_rows)
    missing = bound * (2 * bound + 1) - lax.psum(offsets, "col")
    skipped = missing + jnp.arange(row_count, dtype=jnp.int32)

    sites = jnp.stack([2 * parity + core, 2 * (1 - parity) + core, 2 * parity + 1 - core, 2 * (1 - parity) + 1 - core])
    sites = jnp.concatenate([sites * quarter, jnp.zeros((1,), jnp.int32)]).astype(jnp.int32)
    pieces = [flat, *arrived, from_left, from_right, other, other_left, other_right]
    at = [(d + REACH) * panel for d in SHIFTS]
    layout = [[(0, REACH * panel, 4, panel)]]
    layout += [[(0, t, 0, quarter)] for t in at]
    layout += [[(j * eighth, t, 1, eighth) for j, t in enumerate(at)]]
    layout += [[(j * eighth, t + eighth, 1, eighth) for j, t in enumerate(at)]]
    layout += [[(j * (quarter + 16), t, 2, quarter) for j, t in enumerate(at)]]
    layout += [[(j * eighth, t, 3, eighth) for j, t in enumerate(at)]]
    layout += [[(j * eighth, t + eighth, 3, eighth) for j, t in enumerate(at)]]
    return call_kernel(layout, bs, slots, row_count, sites, window_cols, wanted, skipped, pieces)


def call_kernel(layout, bs, slots, row_count, sites, window_cols, wanted, skipped, pieces):
    window_rows = (2 * REACH + 1) * row_count * slots * bs
    smem = pl.BlockSpec(memory_space=pltpu.SMEM)
    return pl.pallas_call(
        lambda *refs: purify_kernel(layout, bs, slots, *refs),
        out_shape=jax.ShapeDtypeStruct((row_count, 1, bs, bs), jnp.bfloat16),
        in_specs=[smem] * 4 + [pl.BlockSpec(memory_space=pl.ANY)] * len(pieces),
        out_specs=pl.BlockSpec(memory_space=pltpu.VMEM),
        scratch_shapes=[
            pltpu.VMEM((window_rows + bs, bs), jnp.bfloat16),
            pltpu.SMEM((row_count * 32,), jnp.int32),
            pltpu.SemaphoreType.DMA((sum(map(len, layout)),)),
        ],
        compiler_params=pltpu.CompilerParams(vmem_limit_bytes=24 * 2**20),
        name="purify",
    )(sites, window_cols, wanted, skipped, *pieces)


def solution(mesh):
    placed = (P("blk", None, None, None), P("blk", None), P("blk", "col"))
    return jax.shard_map(
        body, mesh=mesh, in_specs=placed, out_specs=P("blk", "col", None, None), check_vma=False
    )
```

time: 497 us -> 78.7 us (0.16)
  waiting for transfers between devices: 246 us -> 1.98 us
  local copies, waits for them, and re-layouts: 87.6 us -> 1.44 us
  blocking collectives: 50 us -> 15.7 us
  matrix products: 25.9 us -> 0 us
  other arithmetic: 27.9 us -> 2.05 us
  between operations: 13.5 us -> 0.23 us
  starting transfers between devices: 43.2 us -> 50.1 us
  Pallas kernels: 0 us -> 6.08 us
    ppermute x10 -> x9, waiting for transfers between devices: 210 us -> 1.98 us  [the longest x5 1.97 us: from_col(): return lax.ppermute(array, 'col', [(source_of(i), i) for i in range(n)])]
    gather x40 -> x0, local copies, waits for them, and re-layouts: 60.3 us -> none  [the longest x16 50.6 us: select_blocks(): picked = window_blocks[located[None, :], position]]
    all_gather x1 -> x0, blocking collectives: 50 us -> none  [body(): lax.all_gather(out_cols, 'col', axis=1, tiled=True)]
    all_gather x1 -> x0, waiting for transfers between devices: 35.8 us -> none  [body(): lax.all_gather(own_squared, 'col', axis=1, tiled=True)]
    dot_general x16 -> x0, matrix products: 25.9 us -> none  [the longest x8 16.2 us: cube_one_row(): jnp.einsum('qij,oqjk->oik', squared_row, chosen, preferred_element_type=j...]
    psum x0 -> x1, blocking collectives: none -> 15.7 us  [body(): missing = bound * (2 * bound + 1) - lax.psum(offsets, 'col')]
    reduce_or x16 -> x0, other arithmetic: 11.1 us -> none  [select_blocks(): found = jnp.any(matches, axis=2)]
    dynamic_update_slice x40 -> x0, local copies, waits for them, and re-layouts: 11.1 us -> none  [the longest x16 5.92 us: square_rows(): return lax.map(square_one_row, (blocks, columns, wanted))]
  transfers between devices with their start and end apart: 11 -> 9, of which waited for: 6 -> 2; matrix products, arithmetic and copies ran while one was open for 0% -> 2% of each run, Pallas kernels for 0% -> 0%
where the time goes in v1:
time: 78.7 us; the launch traced here: 77.6 us
  starting transfers between devices  50.1 us (64%)
  blocking collectives  15.7 us (20%)
  Pallas kernels  6.08 us (8%)
  other arithmetic  2.05 us (3%)
  waiting for transfers between devices  1.98 us (3%)
  local copies, waits for them, and re-layouts  1.44 us (2%)
    ppermute x4, starting transfers between devices, from_blk(): lax.ppermute(array, 'blk', [((i + distance) % n, i) for i in range(n)])  28.7 us
    ppermute x5, starting transfers between devices, from_col(): return lax.ppermute(array, 'col', [(source_of(i), i) for i in range(n)])  21.3 us
    psum x1, blocking collectives, body(): missing = bound * (2 * bound + 1) - lax.psum(offsets, 'col')  15.7 us
    pallas_call x1, Pallas kernels, call_kernel(): pl.pallas_call(lambda *refs: purify_kernel(layout, bs, slots, *refs), out...  6.08 us
    ppermute x5, waiting for transfers between devices, from_col(): return lax.ppermute(array, 'col', [(source_of(i), i) for i in range(n)])  1.97 us
  transfers between devices with their start and end apart: 9, of which 2 were waited for; matrix products, arithmetic and copies ran while one was open for 2% of the time, Pallas kernels for 0%

profile of v1, /device:TPU:1, one launch (start us, length us, event | category | flops | bytes accessed | tf_op | source)
XLA Modules:
  0.0 77.6 jit_solution(7256694175586506434)
XLA Ops:
  0.0 0.0 copy-start.1
  0.0 0.7 convert_element_type.18
  0.7 0.1 copy.6
  0.8 0.1 convert_element_type.19
  0.9 1.0 %constant_dynamic-slice_fusion = bf16[1024,128]{1,0:T(8,128)(2,1)S(1)} fusion(bf16[4096,128]{1,0:T(8,128)(2,1)} %bitcast.16, s32[]{:T(128)S(6)} %select_n.37), kind=kLoop, calls=%fused_computation.25 | loop fusion | bytes 524292 | tf_op jit(solution)/shard_map/dynamic_slice | solution.py:106
  1.9 5.3 %collective-permute-start = (bf16[1040,128]{1,0:T(8,128)(2,1)S(1)}, bf16[1040,128]{1,0:T(8,128)(2,1)S(1)}, u32[]{:S(2)}, u32[]{:S(2)}) collective-permute-start(bf16[1040,128]{1,0:T(8,128)(2,1)S(1)} %fusion.1), channel_id=1, source_target_pairs={{960,0},{992,32},{0,64},{32,96},{64,128},{96,160},{128,192},{160,2... | collective-permute-start | bytes 798728 | tf_op jit(solution)/shard_map/ppermute | solution.py:14
  7.2 3.3 %collective-permute-start.1 = (bf16[1040,128]{1,0:T(8,128)(2,1)S(1)}, bf16[1040,128]{1,0:T(8,128)(2,1)S(1)}, u32[]{:S(2)}, u32[]{:S(2)}) collective-permute-start(bf16[1040,128]{1,0:T(8,128)(2,1)S(1)} %fusion.1), channel_id=1, source_target_pairs={{992,0},{0,32},{32,64},{64,96},{96,128},{128,160},{160,192},{192,2... | collective-permute-start | bytes 798728 | tf_op jit(solution)/shard_map/ppermute | solution.py:14
  10.5 15.9 %collective-permute-start.2 = (bf16[1040,128]{1,0:T(8,128)(2,1)S(1)}, bf16[1040,128]{1,0:T(8,128)(2,1)S(1)}, u32[]{:S(2)}, u32[]{:S(2)}) collective-permute-start(bf16[1040,128]{1,0:T(8,128)(2,1)S(1)} %fusion.1), channel_id=1, source_target_pairs={{32,0},{64,32},{96,64},{128,96},{160,128},{192,160},{224,192},{256... | collective-permute-start | bytes 798728 | tf_op jit(solution)/shard_map/ppermute | solution.py:14
  26.4 4.3 %collective-permute-start.3 = (bf16[1040,128]{1,0:T(8,128)(2,1)S(1)}, bf16[1040,128]{1,0:T(8,128)(2,1)S(1)}, u32[]{:S(2)}, u32[]{:S(2)}) collective-permute-start(bf16[1040,128]{1,0:T(8,128)(2,1)S(1)} %fusion.1), channel_id=1, source_target_pairs={{64,0},{96,32},{128,64},{160,96},{192,128},{224,160},{256,192},{28... | collective-permute-start | bytes 798728 | tf_op jit(solution)/shard_map/ppermute | solution.py:14
  30.7 0.0 copy-done.1
  30.7 15.7 %psum.7 = s32[8]{0:T(128)S(1)} all-reduce(s32[8]{0:T(128)S(1)} %get-tuple-element.17), channel_id=1, replica_groups=mesh['blk'=32,'col'=32] {'col'}, use_global_device_ids=true, to_apply=%region_0.1 | all-reduce | flops 8 | bytes 64 | tf_op jit(solution)/shard_map/psum | solution.py:129
  46.5 0.1 add_multiply_fusion
  46.5 0.1 pad_add_fusion.refs_0_
  46.6 0.1 convert_element_type.20
  46.7 0.0 collective-permute-done.2.refs_5_
  46.7 0.0 collective-permute-done.1.refs_6_
  46.8 0.0 collective-permute-done.3.refs_7_
  46.8 0.0 collective-permute-done.refs_8_
  46.9 3.1 %collective-permute-start.5 = (bf16[2048,128]{1,0:T(8,128)(2,1)S(1)}, bf16[2048,128]{1,0:T(8,128)(2,1)}, u32[]{:S(2)}, u32[]{:S(2)}) collective-permute-start(bf16[2048,128]{1,0:T(8,128)(2,1)S(1)} %pad_maximum_fusion.2), channel_id=1, source_target_pairs={{4,0},{5,1},{6,2},{7,3},{8,4},{9,5},{10,6},{11,7},{12,8},{13,9},{1... | collective-permute-start | bytes 1572872 | tf_op jit(solution)/shard_map/ppermute | solution.py:19
  50.0 0.0 copy-start
  50.0 2.3 %collective-permute-start.4 = (bf16[2048,128]{1,0:T(8,128)(2,1)S(1)}, bf16[2048,128]{1,0:T(8,128)(2,1)}, u32[]{:S(2)}, u32[]{:S(2)}) collective-permute-start(bf16[2048,128]{1,0:T(8,128)(2,1)S(1)} %pad_maximum_fusion.1), channel_id=1, source_target_pairs={{28,0},{29,1},{30,2},{31,3},{0,4},{1,5},{2,6},{3,7},{4,8},{5,9},{6... | collective-permute-start | bytes 1572872 | tf_op jit(solution)/shard_map/ppermute | solution.py:19
  52.4 1.1 %pad_maximum_fusion = bf16[4160,128]{1,0:T(8,128)(2,1)} fusion(bf16[1040,128]{1,0:T(8,128)(2,1)S(1)} %collective-permute-done.refs_8_, bf16[1040,128]{1,0:T(8,128)(2,1)S(1)} %collective-permute-done.3.refs_7_, bf16[1040,128]{1,0:T(8,128)(2,1)S(1)} %collective-permute-done.1.refs_6_, bf16[1040,128]{1,0:T(8,128)(2,1)S(1)} %collective-permute-done.2.refs_5_), kind=kLoop, calls=%fused_computation | loop fusion | flops 4259840 | bytes 2129920 | tf_op jit(solution)/shard_map/concatenate | solution.py:115
  53.4 5.5 %collective-permute-start.6 = (bf16[4160,128]{1,0:T(8,128)(2,1)}, bf16[4160,128]{1,0:T(8,128)(2,1)S(1)}, u32[]{:S(2)}, u32[]{:S(2)}) collective-permute-start(bf16[4160,128]{1,0:T(8,128)(2,1)} %pad_maximum_fusion), channel_id=1, source_target_pairs={{1,0},{0,1},{3,2},{2,3},{5,4},{4,5},{7,6},{6,7},{9,8},{8,9},{11,10... | collective-permute-start | bytes 3194888 | tf_op jit(solution)/shard_map/ppermute | solution.py:19
  59.0 0.2 collective-permute-done.5.refs_10_
  59.2 5.9 %collective-permute-start.8 = (bf16[2048,128]{1,0:T(8,128)(2,1)}, bf16[2048,128]{1,0:T(8,128)(2,1)}, u32[]{:S(2)}, u32[]{:S(2)}) collective-permute-start(bf16[2048,128]{1,0:T(8,128)(2,1)} %collective-permute-done.5.refs_10_), channel_id=1, source_target_pairs={{1,0},{0,1},{3,2},{2,3},{5,4},{4,5},{7,6},{6,7},{9,8},{8,9},{11,10... | collective-permute-start | bytes 1572872 | tf_op jit(solution)/shard_map/ppermute | solution.py:19
  65.1 0.0 collective-permute-done.4.refs_9_
  65.1 4.5 %collective-permute-start.7 = (bf16[2048,128]{1,0:T(8,128)(2,1)}, bf16[2048,128]{1,0:T(8,128)(2,1)}, u32[]{:S(2)}, u32[]{:S(2)}) collective-permute-start(bf16[2048,128]{1,0:T(8,128)(2,1)} %collective-permute-done.4.refs_9_), channel_id=1, source_target_pairs={{1,0},{0,1},{3,2},{2,3},{5,4},{4,5},{7,6},{6,7},{9,8},{8,9},{11,10... | collective-permute-start | bytes 1572872 | tf_op jit(solution)/shard_map/ppermute | solution.py:19
  69.7 0.1 concatenate.22
  69.8 0.0 collective-permute-done.8.refs_13_
  69.8 1.7 %collective-permute-done.7.refs_12_ = bf16[2048,128]{1,0:T(8,128)(2,1)} collective-permute-done((bf16[2048,128]{1,0:T(8,128)(2,1)}, bf16[2048,128]{1,0:T(8,128)(2,1)}, u32[]{:S(2)}, u32[]{:S(2)}) %collective-permute-start.7) | collective-permute-done | bytes 524320 | tf_op jit(solution)/shard_map/ppermute | solution.py:19
  71.5 0.0 collective-permute-done.6.refs_11_
  71.5 0.0 copy-done
  71.5 6.1 %purify.1 = bf16[8,1,128,128]{3,2,1,0:T(8,128)(2,1)} custom-call(s32[5]{0:T(128)S(1)} %pad_add_fusion.refs_0_, s32[160]{0:T(256)S(1)} %and_select_fusion.2.refs_1_, s32[8]{0:T(128)S(1)} %get-tuple-element.18.refs_2_, s32[8]{0:T(128)S(1)} %iota_add_fusion.refs_3_, bf16[4096,128]{1,0:T(8,128)(2,1)S(1)} %bitcast.17, ...), custom_call_target="tpu_custom_call" | custom-call | tf_op jit(solution)/shard_map/purify/pallas_call | solution.py:149
  (14 shorter events, 0.2 us)
Async XLA Ops:
  0.0 30.7 %copy-start.1 = (s32[8,1]{0,1:T(1,128)S(1)}, s32[8,1]{0,1:T(1,128)}, u32[]{:S(2)}) copy-start(s32[8,1]{0,1:T(1,128)} %param.7) | copy-start | bytes 100
  1.9 44.9 %collective-permute-start = (bf16[1040,128]{1,0:T(8,128)(2,1)S(1)}, bf16[1040,128]{1,0:T(8,128)(2,1)S(1)}, u32[]{:S(2)}, u32[]{:S(2)}) collective-permute-start(bf16[1040,128]{1,0:T(8,128)(2,1)S(1)} %fusion.1), channel_id=1, source_target_pairs={{960,0},{992,32},{0,64},{32,96},{64,128},{96,160},{128,192},{160,2... | collective-permute-start | bytes 798728 | tf_op jit(solution)/shard_map/ppermute | solution.py:14
  7.2 39.6 %collective-permute-start.1 = (bf16[1040,128]{1,0:T(8,128)(2,1)S(1)}, bf16[1040,128]{1,0:T(8,128)(2,1)S(1)}, u32[]{:S(2)}, u32[]{:S(2)}) collective-permute-start(bf16[1040,128]{1,0:T(8,128)(2,1)S(1)} %fusion.1), channel_id=1, source_target_pairs={{992,0},{0,32},{32,64},{64,96},{96,128},{128,160},{160,192},{192,2... | collective-permute-start | bytes 798728 | tf_op jit(solution)/shard_map/ppermute | solution.py:14
  10.5 36.2 %collective-permute-start.2 = (bf16[1040,128]{1,0:T(8,128)(2,1)S(1)}, bf16[1040,128]{1,0:T(8,128)(2,1)S(1)}, u32[]{:S(2)}, u32[]{:S(2)}) collective-permute-start(bf16[1040,128]{1,0:T(8,128)(2,1)S(1)} %fusion.1), channel_id=1, source_target_pairs={{32,0},{64,32},{96,64},{128,96},{160,128},{192,160},{224,192},{256... | collective-permute-start | bytes 798728 | tf_op jit(solution)/shard_map/ppermute | solution.py:14
  26.4 20.4 %collective-permute-start.3 = (bf16[1040,128]{1,0:T(8,128)(2,1)S(1)}, bf16[1040,128]{1,0:T(8,128)(2,1)S(1)}, u32[]{:S(2)}, u32[]{:S(2)}) collective-permute-start(bf16[1040,128]{1,0:T(8,128)(2,1)S(1)} %fusion.1), channel_id=1, source_target_pairs={{64,0},{96,32},{128,64},{160,96},{192,128},{224,160},{256,192},{28... | collective-permute-start | bytes 798728 | tf_op jit(solution)/shard_map/ppermute | solution.py:14
  46.9 12.3 %collective-permute-start.5 = (bf16[2048,128]{1,0:T(8,128)(2,1)S(1)}, bf16[2048,128]{1,0:T(8,128)(2,1)}, u32[]{:S(2)}, u32[]{:S(2)}) collective-permute-start(bf16[2048,128]{1,0:T(8,128)(2,1)S(1)} %pad_maximum_fusion.2), channel_id=1, source_target_pairs={{4,0},{5,1},{6,2},{7,3},{8,4},{9,5},{10,6},{11,7},{12,8},{13,9},{1... | collective-permute-start | bytes 1572872 | tf_op jit(solution)/shard_map/ppermute | solution.py:19
  50.0 21.5 %copy-start = (bf16[8,4,128,128]{3,2,1,0:T(8,128)(2,1)S(1)}, bf16[8,4,128,128]{3,2,1,0:T(8,128)(2,1)}, u32[]{:S(2)}) copy-start(bf16[8,4,128,128]{3,2,1,0:T(8,128)(2,1)} %param.5) | copy-start | bytes 3145732
  50.0 15.1 %collective-permute-start.4 = (bf16[2048,128]{1,0:T(8,128)(2,1)S(1)}, bf16[2048,128]{1,0:T(8,128)(2,1)}, u32[]{:S(2)}, u32[]{:S(2)}) collective-permute-start(bf16[2048,128]{1,0:T(8,128)(2,1)S(1)} %pad_maximum_fusion.1), channel_id=1, source_target_pairs={{28,0},{29,1},{30,2},{31,3},{0,4},{1,5},{2,6},{3,7},{4,8},{5,9},{6... | collective-permute-start | bytes 1572872 | tf_op jit(solution)/shard_map/ppermute | solution.py:19
  53.4 18.1 %collective-permute-start.6 = (bf16[4160,128]{1,0:T(8,128)(2,1)}, bf16[4160,128]{1,0:T(8,128)(2,1)S(1)}, u32[]{:S(2)}, u32[]{:S(2)}) collective-permute-start(bf16[4160,128]{1,0:T(8,128)(2,1)} %pad_maximum_fusion), channel_id=1, source_target_pairs={{1,0},{0,1},{3,2},{2,3},{5,4},{4,5},{7,6},{6,7},{9,8},{8,9},{11,10... | collective-permute-start | bytes 3194888 | tf_op jit(solution)/shard_map/ppermute | solution.py:19
  59.2 10.5 %collective-permute-start.8 = (bf16[2048,128]{1,0:T(8,128)(2,1)}, bf16[2048,128]{1,0:T(8,128)(2,1)}, u32[]{:S(2)}, u32[]{:S(2)}) collective-permute-start(bf16[2048,128]{1,0:T(8,128)(2,1)} %collective-permute-done.5.refs_10_), channel_id=1, source_target_pairs={{1,0},{0,1},{3,2},{2,3},{5,4},{4,5},{7,6},{6,7},{9,8},{8,9},{11,10... | collective-permute-start | bytes 1572872 | tf_op jit(solution)/shard_map/ppermute | solution.py:19
  65.1 6.3 %collective-permute-start.7 = (bf16[2048,128]{1,0:T(8,128)(2,1)}, bf16[2048,128]{1,0:T(8,128)(2,1)}, u32[]{:S(2)}, u32[]{:S(2)}) collective-permute-start(bf16[2048,128]{1,0:T(8,128)(2,1)} %collective-permute-done.4.refs_9_), channel_id=1, source_target_pairs={{1,0},{0,1},{3,2},{2,3},{5,4},{4,5},{7,6},{6,7},{9,8},{8,9},{11,10... | collective-permute-start | bytes 1572872 | tf_op jit(solution)/shard_map/ppermute | solution.py:19

commit v2 on v1

--- a/solution.py
+++ b/solution.py
@@ -6,29 +6,22 @@
 from jax.sharding import PartitionSpec as P
 
 REACH = 2
-SHIFTS = (1, -1, 2, -2)
+def swap_routes(partner_of):
+    return [(partner_of(i), i) for i in range(lax.axis_size("blk"))]
 
 
-def from_blk(array, distance):
-    n = lax.axis_size("blk")
-    return lax.ppermute(array, "blk", [((i + distance) % n, i) for i in range(n)])
+def col_routes(source_of):
+    return [(source_of(i) % lax.axis_size("col"), i) for i in range(lax.axis_size("col"))]
 
 
-def from_col(array, source_of):
-    n = lax.axis_size("col")
-    return lax.ppermute(array, "col", [(source_of(i), i) for i in range(n)])
-
-
-def purify_kernel(
-    layout, bs, slots, sites_ref, cols_ref, wanted_ref, skipped_ref, *refs
-):
+def purify_kernel(layout, bs, slots, targets_ref, cols_ref, wanted_ref, skipped_ref, *refs):
     pieces, out_ref, window, picks, sems = refs[:-4], refs[-4], refs[-3], refs[-2], refs[-1]
     row_count = out_ref.shape[0]
     nothing = window.shape[0] // bs - 1
     copies = []
     for ref, moves in zip(pieces, layout, strict=True):
-        for source, target, site, rows in moves:
-            start = pl.multiple_of(target + sites_ref[site], bs)
+        for source, rows in moves:
+            start = pl.multiple_of(targets_ref[len(copies)], bs)
             copies.append(
                 pltpu.make_async_copy(
                     ref.at[pl.ds(source, rows)],
@@ -95,57 +88,74 @@
     own = lax.axis_index("blk")
     place = lax.axis_index("col")
     window_start = (own - REACH) * row_count
-
-    parity, core = (place // 4) % 2, place % 2
-    mine = 2 * parity + core
+    parity, core = jnp.bitwise_and(place >> 2, 1), jnp.bitwise_and(place, 1)
     flat = pvals.reshape(panel, bs)
     own_cols = pcols.reshape(-1)
     tail = jnp.zeros((16, bs), jnp.bfloat16)
     tail = tail.at[0, : own_cols.shape[0]].set(own_cols.astype(jnp.bfloat16))
-    parcel = jnp.concatenate(
-        [lax.dynamic_slice_in_dim(flat, mine * quarter, quarter, 0), tail], 0
-    )
-    arrived = [from_blk(parcel, d) for d in SHIFTS]
-    from_left = from_col(
-        jnp.concatenate([x[:eighth] for x in arrived], 0), lambda i: (i - 4) % 32
-    )
-    from_right = from_col(
-        jnp.concatenate([x[eighth:quarter] for x in arrived], 0), lambda i: (i + 4) % 32
-    )
-    other = from_col(jnp.concatenate(arrived, 0), lambda i: i ^ 1)
-    other_left = from_col(from_left, lambda i: i ^ 1)
-    other_right = from_col(from_right, lambda i: i ^ 1)
+    mine = lax.dynamic_slice_in_dim(flat, (2 * parity + core) * quarter, quarter, 0)
+    parcel = jnp.concatenate([mine, tail], 0)
+
+    count = lax.axis_size("blk")
+    late = [
+        lax.ppermute(parcel, "blk", swap_routes(lambda i, d=d: (((i + d) ^ d) - d) % count))
+        for d in (1, 2)
+    ]
+    early = [lax.ppermute(parcel, "blk", swap_routes(lambda i, d=d: i ^ d)) for d in (1, 2)]
+
+    def spread(arrived):
+        left = lax.ppermute(
+            jnp.concatenate([x[:eighth] for x in arrived], 0), "col", col_routes(lambda i: i - 4)
+        )
+        right = lax.ppermute(
+            jnp.concatenate([x[eighth:quarter] for x in arrived], 0), "col", col_routes(lambda i: i + 4)
+        )
+        other = lax.ppermute(jnp.concatenate(arrived, 0), "col", col_routes(lambda i: i ^ 1))
+        sides = lax.ppermute(jnp.concatenate([left, right], 0), "col", col_routes(lambda i: i ^ 1))
+        return [*arrived, left, right, other, sides]
 
     def local(ids):
-        return jnp.mod(ids - window_start, total_rows).astype(jnp.int32)
+        return jnp.bitwise_and(ids - window_start, total_rows - 1).astype(jnp.int32)
 
-    by_shift = {d: x[quarter, : own_cols.shape[0]] for d, x in zip(SHIFTS, arrived)}
-    by_shift[0] = own_cols.astype(jnp.bfloat16)
-    window_cols = jnp.concatenate([by_shift[d] for d in range(-REACH, REACH + 1)])
+    def listed(x):
+        return x[quarter, : own_cols.shape[0]]
+
+    odd = [jnp.bitwise_and(own, d) != 0 for d in (1, 2)]
+    ahead = [jnp.where(o, listed(x), listed(y)) for o, x, y in zip(odd, late, early)]
+    behind = [jnp.where(o, listed(y), listed(x)) for o, x, y in zip(odd, late, early)]
+    window_cols = jnp.concatenate(
+        [behind[1], behind[0], own_cols.astype(jnp.bfloat16), ahead[0], ahead[1]]
+    )
     window_cols = local(window_cols.astype(jnp.int32))
     wanted = local(out_cols[:, 0])
     bound = REACH * row_count
-    offsets = jnp.mod(wanted - jnp.arange(row_count), total_rows)
-    missing = bound * (2 * bound + 1) - lax.psum(offsets, "col")
-    skipped = missing + jnp.arange(row_count, dtype=jnp.int32)
+    rows = jnp.arange(row_count, dtype=jnp.int32)
+    offsets = jnp.bitwise_and(wanted - rows, total_rows - 1)
+    skipped = bound * (2 * bound + 1) - lax.psum(offsets, "col") + rows
 
-    sites = jnp.stack([2 * parity + core, 2 * (1 - parity) + core, 2 * parity + 1 - core, 2 * (1 - parity) + 1 - core])
-    sites = jnp.concatenate([sites * quarter, jnp.zeros((1,), jnp.int32)]).astype(jnp.int32)
-    pieces = [flat, *arrived, from_left, from_right, other, other_left, other_right]
-    at = [(d + REACH) * panel for d in SHIFTS]
-    layout = [[(0, REACH * panel, 4, panel)]]
-    layout += [[(0, t, 0, quarter)] for t in at]
-    layout += [[(j * eighth, t, 1, eighth) for j, t in enumerate(at)]]
-    layout += [[(j * eighth, t + eighth, 1, eighth) for j, t in enumerate(at)]]
-    layout += [[(j * (quarter + 16), t, 2, quarter) for j, t in enumerate(at)]]
-    layout += [[(j * eighth, t, 3, eighth) for j, t in enumerate(at)]]
-    layout += [[(j * eighth, t + eighth, 3, eighth) for j, t in enumerate(at)]]
-    return call_kernel(layout, bs, slots, row_count, sites, window_cols, wanted, skipped, pieces)
+    early_pieces = spread(early)
+    late, early_pieces[2:4] = lax.optimization_barrier((late, early_pieces[2:4]))
+    pieces = [flat] + early_pieces + spread(late)
+    site = {
+        (h, c): (2 * (parity ^ h) + (core ^ c)) * quarter for h in (0, 1) for c in (0, 1)
+    }
+    layout, targets = [[(0, panel)]], [jnp.int32(REACH * panel)]
+    for way in (1, -1):
+        tops = [(REACH + jnp.where(o, -way, way) * d) * panel for o, d in zip(odd, (1, 2))]
+        for top in tops:
+            layout.append([(0, quarter)])
+            targets.append(top + site[0, 0])
+        for shift in (0, eighth):
+            layout.append([(0, eighth), (eighth, eighth)])
+            targets += [top + site[1, 0] + shift for top in tops]
+        layout.append([(0, quarter), (quarter + 16, quarter)])
+        targets += [top + site[0, 1] for top in tops]
+        layout.append([(j * eighth, eighth) for j in range(4)])
+        targets += [top + site[1, 1] + shift for shift in (0, eighth) for top in tops]
+    targets = jnp.stack(targets).astype(jnp.int32)
 
-
-def call_kernel(layout, bs, slots, row_count, sites, window_cols, wanted, skipped, pieces):
-    window_rows = (2 * REACH + 1) * row_count * slots * bs
     smem = pl.BlockSpec(memory_space=pltpu.SMEM)
+    window_rows = (2 * REACH + 1) * panel
     return pl.pallas_call(
         lambda *refs: purify_kernel(layout, bs, slots, *refs),
         out_shape=jax.ShapeDtypeStruct((row_count, 1, bs, bs), jnp.bfloat16),
@@ -156,9 +166,9 @@
             pltpu.SMEM((row_count * 32,), jnp.int32),
             pltpu.SemaphoreType.DMA((sum(map(len, layout)),)),
         ],
-        compiler_params=pltpu.CompilerParams(vmem_limit_bytes=24 * 2**20),
+        compiler_params=pltpu.CompilerParams(vmem_limit_bytes=10 * 2**20),
         name="purify",
-    )(sites, window_cols, wanted, skipped, *pieces)
+    )(targets, window_cols, wanted, skipped, *pieces)
 
 
 def solution(mesh):

time: 78.7 us -> 91.6 us (1.16)
  starting transfers between devices: 50.1 us -> 57.5 us
  waiting for transfers between devices: 1.98 us -> 4.46 us
  other arithmetic: 2.05 us -> 4.19 us
  Pallas kernels: 6.08 us -> 7.1 us
    ppermute x9 -> x12, starting transfers between devices: 50.1 us -> 57.5 us  [the longest x2 24.9 us: body(): lax.ppermute(parcel, 'blk', swap_routes(lambda i, d=d: ((i + d ^ d) - d)...]
    ppermute x9 -> x12, waiting for transfers between devices: 1.98 us -> 4.46 us  [the longest x2 1.7 us: spread(): lax.ppermute(jnp.concatenate([left, right], 0), 'col', col_routes(lambda...]
    concatenate x5 -> x9, other arithmetic: 1.23 us -> 3.46 us  [the longest x2 1.72 us: spread(): jnp.concatenate(arrived, 0)]
    pallas_call x1, Pallas kernels: 6.08 us -> 7.1 us  [body(): pl.pallas_call(lambda *refs: purify_kernel(layout, bs, slots, *refs), out...]
  transfers between devices with their start and end apart: 9 -> 12, of which waited for: 2 -> 3; matrix products, arithmetic and copies ran while one was open for 2% -> 4% of each run, Pallas kernels for 0% -> 0%
where the time goes in v2:
time: 91.6 us; the launch traced here: 91.1 us
  starting transfers between devices  57.5 us (63%)
  blocking collectives  16 us (17%)
  Pallas kernels  7.1 us (8%)
  waiting for transfers between devices  4.46 us (5%)
  other arithmetic  4.19 us (5%)
  local copies, waits for them, and re-layouts  1.53 us (2%)
    ppermute x2, starting transfers between devices, body(): lax.ppermute(parcel, 'blk', swap_routes(lambda i, d=d: ((i + d ^ d) - d)...  24.9 us
    psum x1, blocking collectives, body(): skipped = bound * (2 * bound + 1) - lax.psum(offsets, 'col') + rows  16 us
    ppermute x2, starting transfers between devices, spread(): lax.ppermute(jnp.concatenate(arrived, 0), 'col', col_routes(lambda i: i ^...  7.93 us
    pallas_call x1, Pallas kernels, body(): pl.pallas_call(lambda *refs: purify_kernel(layout, bs, slots, *refs), out...  7.1 us
    ppermute x2, starting transfers between devices, spread(): lax.ppermute(jnp.concatenate([x[eighth:quarter] for x in arrived], 0), 'c...  7 us
    ppermute x2, starting transfers between devices, spread(): lax.ppermute(jnp.concatenate([left, right], 0), 'col', col_routes(lambda...  6.69 us
    ppermute x2, starting transfers between devices, spread(): lax.ppermute(jnp.concatenate([x[:eighth] for x in arrived], 0), 'col', co...  6.14 us
    ppermute x2, starting transfers between devices, body(): lax.ppermute(parcel, 'blk', swap_routes(lambda i, d=d: i ^ d))  4.79 us
  transfers between devices with their start and end apart: 12, of which 3 were waited for; matrix products, arithmetic and copies ran while one was open for 4% of the time, Pallas kernels for 0%

profile of v2, /device:TPU:1, one launch (start us, length us, event | category | flops | bytes accessed | tf_op | source)
XLA Modules:
  0.0 91.1 jit_solution(18047109436023179708)
XLA Ops:
  0.0 0.0 copy-start.1
  0.0 0.7 convert_element_type.18
  0.7 0.1 copy.6
  0.8 0.1 convert_element_type.19
  0.9 1.0 %constant_dynamic-slice_fusion = bf16[1024,128]{1,0:T(8,128)(2,1)S(1)} fusion(bf16[4096,128]{1,0:T(8,128)(2,1)} %bitcast.36, s32[]{:T(128)S(6)} %select_n.55), kind=kLoop, calls=%fused_computation.23 | loop fusion | bytes 524292 | tf_op jit(solution)/shard_map/dynamic_slice | solution.py:96
  1.9 21.3 %collective-permute-start.1 = (bf16[1040,128]{1,0:T(8,128)(2,1)S(1)}, bf16[1040,128]{1,0:T(8,128)(2,1)S(1)}, u32[]{:S(2)}, u32[]{:S(2)}) collective-permute-start(bf16[1040,128]{1,0:T(8,128)(2,1)S(1)} %fusion.1), channel_id=1, source_target_pairs={{960,0},{992,32},{128,64},{160,96},{64,128},{96,160},{256,192},{28... | collective-permute-start | bytes 798728 | tf_op jit(solution)/shard_map/ppermute | solution.py:101
  23.2 1.9 %collective-permute-start = (bf16[1040,128]{1,0:T(8,128)(2,1)S(1)}, bf16[1040,128]{1,0:T(8,128)(2,1)S(1)}, u32[]{:S(2)}, u32[]{:S(2)}) collective-permute-start(bf16[1040,128]{1,0:T(8,128)(2,1)S(1)} %fusion.1), channel_id=1, source_target_pairs={{64,0},{96,32},{0,64},{32,96},{192,128},{224,160},{128,192},{160,2... | collective-permute-start | bytes 798728 | tf_op jit(solution)/shard_map/ppermute | solution.py:104
  25.1 3.6 %collective-permute-start.3 = (bf16[1040,128]{1,0:T(8,128)(2,1)S(1)}, bf16[1040,128]{1,0:T(8,128)(2,1)S(1)}, u32[]{:S(2)}, u32[]{:S(2)}) collective-permute-start(bf16[1040,128]{1,0:T(8,128)(2,1)S(1)} %fusion.1), channel_id=1, source_target_pairs={{992,0},{64,32},{32,64},{128,96},{96,128},{192,160},{160,192},{256... | collective-permute-start | bytes 798728 | tf_op jit(solution)/shard_map/ppermute | solution.py:101
  28.7 2.9 %collective-permute-start.2 = (bf16[1040,128]{1,0:T(8,128)(2,1)S(1)}, bf16[1040,128]{1,0:T(8,128)(2,1)S(1)}, u32[]{:S(2)}, u32[]{:S(2)}) collective-permute-start(bf16[1040,128]{1,0:T(8,128)(2,1)S(1)} %fusion.1), channel_id=1, source_target_pairs={{32,0},{0,32},{96,64},{64,96},{160,128},{128,160},{224,192},{192,2... | collective-permute-start | bytes 798728 | tf_op jit(solution)/shard_map/ppermute | solution.py:104
  31.6 0.0 copy-done.1
  31.6 16.0 %psum.7 = s32[8]{0:T(128)S(1)} all-reduce(s32[8]{0:T(128)S(1)} %get-tuple-element.25), channel_id=1, replica_groups=mesh['blk'=32,'col'=32] {'col'}, use_global_device_ids=true, to_apply=%region_0.0 | all-reduce | flops 8 | bytes 64 | tf_op jit(solution)/shard_map/psum | solution.py:134
  47.7 0.1 convert_element_type.20
  47.8 0.1 stack.99.refs_0_
  47.9 0.0 collective-permute-done.refs_6_
  47.9 0.0 collective-permute-done.2.refs_5_
  48.0 3.1 %collective-permute-start.4 = (bf16[1024,128]{1,0:T(8,128)(2,1)S(1)}, bf16[1024,128]{1,0:T(8,128)(2,1)S(1)}, u32[]{:S(2)}, u32[]{:S(2)}) collective-permute-start(bf16[1024,128]{1,0:T(8,128)(2,1)S(1)} %pad_maximum_fusion.4), channel_id=1, source_target_pairs={{28,0},{29,1},{30,2},{31,3},{0,4},{1,5},{2,6},{3,7},{4,8},{5,9},{6... | collective-permute-start | bytes 786440 | tf_op jit(solution)/shard_map/ppermute | solution.py:107
  51.1 3.4 %collective-permute-start.5 = (bf16[1024,128]{1,0:T(8,128)(2,1)S(1)}, bf16[1024,128]{1,0:T(8,128)(2,1)S(1)}, u32[]{:S(2)}, u32[]{:S(2)}) collective-permute-start(bf16[1024,128]{1,0:T(8,128)(2,1)S(1)} %pad_maximum_fusion.5), channel_id=1, source_target_pairs={{4,0},{5,1},{6,2},{7,3},{8,4},{9,5},{10,6},{11,7},{12,8},{13,9},{1... | collective-permute-start | bytes 786440 | tf_op jit(solution)/shard_map/ppermute | solution.py:110
  54.5 0.9 pad_maximum_fusion
  55.4 5.5 %collective-permute-start.6 = (bf16[2080,128]{1,0:T(8,128)(2,1)}, bf16[2080,128]{1,0:T(8,128)(2,1)}, u32[]{:S(2)}, u32[]{:S(2)}) collective-permute-start(bf16[2080,128]{1,0:T(8,128)(2,1)} %pad_maximum_fusion), channel_id=1, source_target_pairs={{1,0},{0,1},{3,2},{2,3},{5,4},{4,5},{7,6},{6,7},{9,8},{8,9},{11,10... | collective-permute-start | bytes 1597448 | tf_op jit(solution)/shard_map/ppermute | solution.py:113
  60.9 0.0 collective-permute-done.1.refs_12_
  60.9 0.0 collective-permute-done.3.refs_11_
  60.9 0.0 collective-permute-done.4.refs_7_
  60.9 0.0 collective-permute-done.5.refs_8_
  60.9 0.8 pad_maximum_fusion.2
  61.8 3.7 %collective-permute-start.7 = (bf16[2048,128]{1,0:T(8,128)(2,1)}, bf16[2048,128]{1,0:T(8,128)(2,1)}, u32[]{:S(2)}, u32[]{:S(2)}) collective-permute-start(bf16[2048,128]{1,0:T(8,128)(2,1)} %pad_maximum_fusion.2), channel_id=1, source_target_pairs={{1,0},{0,1},{3,2},{2,3},{5,4},{4,5},{7,6},{6,7},{9,8},{8,9},{11,10... | collective-permute-start | bytes 1572872 | tf_op jit(solution)/shard_map/ppermute | solution.py:114
  65.5 3.1 %collective-permute-start.8 = (bf16[1024,128]{1,0:T(8,128)(2,1)S(1)}, bf16[1024,128]{1,0:T(8,128)(2,1)S(1)}, u32[]{:S(2)}, u32[]{:S(2)}) collective-permute-start(bf16[1024,128]{1,0:T(8,128)(2,1)S(1)} %pad_maximum_fusion.6), channel_id=1, source_target_pairs={{28,0},{29,1},{30,2},{31,3},{0,4},{1,5},{2,6},{3,7},{4,8},{5,9},{6... | collective-permute-start | bytes 786440 | tf_op jit(solution)/shard_map/ppermute | solution.py:107
  68.6 0.0 copy-start
  68.7 3.6 %collective-permute-start.9 = (bf16[1024,128]{1,0:T(8,128)(2,1)S(1)}, bf16[1024,128]{1,0:T(8,128)(2,1)S(1)}, u32[]{:S(2)}, u32[]{:S(2)}) collective-permute-start(bf16[1024,128]{1,0:T(8,128)(2,1)S(1)} %pad_maximum_fusion.7), channel_id=1, source_target_pairs={{4,0},{5,1},{6,2},{7,3},{8,4},{9,5},{10,6},{11,7},{12,8},{13,9},{1... | collective-permute-start | bytes 786440 | tf_op jit(solution)/shard_map/ppermute | solution.py:110
  72.2 0.9 pad_maximum_fusion.1
  73.1 2.4 %collective-permute-start.10 = (bf16[2080,128]{1,0:T(8,128)(2,1)}, bf16[2080,128]{1,0:T(8,128)(2,1)}, u32[]{:S(2)}, u32[]{:S(2)}) collective-permute-start(bf16[2080,128]{1,0:T(8,128)(2,1)} %pad_maximum_fusion.1), channel_id=1, source_target_pairs={{1,0},{0,1},{3,2},{2,3},{5,4},{4,5},{7,6},{6,7},{9,8},{8,9},{11,10... | collective-permute-start | bytes 1597448 | tf_op jit(solution)/shard_map/ppermute | solution.py:113
  75.5 1.1 %collective-permute-done.8.refs_13_ = bf16[1024,128]{1,0:T(8,128)(2,1)S(1)} collective-permute-done((bf16[1024,128]{1,0:T(8,128)(2,1)S(1)}, bf16[1024,128]{1,0:T(8,128)(2,1)S(1)}, u32[]{:S(2)}, u32[]{:S(2)}) %collective-permute-start.8) | collective-permute-done | bytes 262176 | tf_op jit(solution)/shard_map/ppermute | solution.py:107
  76.6 1.7 %collective-permute-done.9.refs_14_ = bf16[1024,128]{1,0:T(8,128)(2,1)S(1)} collective-permute-done((bf16[1024,128]{1,0:T(8,128)(2,1)S(1)}, bf16[1024,128]{1,0:T(8,128)(2,1)S(1)}, u32[]{:S(2)}, u32[]{:S(2)}) %collective-permute-start.9) | collective-permute-done | bytes 262176 | tf_op jit(solution)/shard_map/ppermute | solution.py:110
  78.3 0.8 pad_maximum_fusion.3
  79.1 3.0 %collective-permute-start.11 = (bf16[2048,128]{1,0:T(8,128)(2,1)}, bf16[2048,128]{1,0:T(8,128)(2,1)}, u32[]{:S(2)}, u32[]{:S(2)}) collective-permute-start(bf16[2048,128]{1,0:T(8,128)(2,1)} %pad_maximum_fusion.3), channel_id=1, source_target_pairs={{1,0},{0,1},{3,2},{2,3},{5,4},{4,5},{7,6},{6,7},{9,8},{8,9},{11,10... | collective-permute-start | bytes 1572872 | tf_op jit(solution)/shard_map/ppermute | solution.py:114
  82.2 0.1 concatenate.33
  82.3 0.0 collective-permute-done.6.refs_9_
  82.3 0.0 collective-permute-done.7.refs_10_
  82.3 0.0 collective-permute-done.10.refs_15_
  82.3 1.7 %collective-permute-done.11.refs_16_ = bf16[2048,128]{1,0:T(8,128)(2,1)} collective-permute-done((bf16[2048,128]{1,0:T(8,128)(2,1)}, bf16[2048,128]{1,0:T(8,128)(2,1)}, u32[]{:S(2)}, u32[]{:S(2)}) %collective-permute-start.11) | collective-permute-done | bytes 524320 | tf_op jit(solution)/shard_map/ppermute | solution.py:114
  84.0 0.0 copy-done
  84.0 7.1 %purify.1 = bf16[8,1,128,128]{3,2,1,0:T(8,128)(2,1)} custom-call(s32[25]{0:T(128)S(1)} %stack.99.refs_0_, s32[160]{0:T(256)S(1)} %subtract_and_fusion.refs_1_, s32[8]{0:T(128)S(1)} %get-tuple-element.26.refs_2_, s32[8]{0:T(128)S(1)} %iota_add_fusion.refs_3_, bf16[4096,128]{1,0:T(8,128)(2,1)S(1)} %bitcast.37, ...), custom_call_target="tpu_custom_call" | custom-call | tf_op jit(solution)/shard_map/purify/pallas_call | solution.py:159
  (13 shorter events, 0.2 us)
Async XLA Ops:
  0.0 31.6 %copy-start.1 = (s32[8,1]{0,1:T(1,128)S(1)}, s32[8,1]{0,1:T(1,128)}, u32[]{:S(2)}) copy-start(s32[8,1]{0,1:T(1,128)} %param.7) | copy-start | bytes 100
  1.9 59.0 %collective-permute-start.1 = (bf16[1040,128]{1,0:T(8,128)(2,1)S(1)}, bf16[1040,128]{1,0:T(8,128)(2,1)S(1)}, u32[]{:S(2)}, u32[]{:S(2)}) collective-permute-start(bf16[1040,128]{1,0:T(8,128)(2,1)S(1)} %fusion.1), channel_id=1, source_target_pairs={{960,0},{992,32},{128,64},{160,96},{64,128},{96,160},{256,192},{28... | collective-permute-start | bytes 798728 | tf_op jit(solution)/shard_map/ppermute | solution.py:101
  23.2 24.7 %collective-permute-start = (bf16[1040,128]{1,0:T(8,128)(2,1)S(1)}, bf16[1040,128]{1,0:T(8,128)(2,1)S(1)}, u32[]{:S(2)}, u32[]{:S(2)}) collective-permute-start(bf16[1040,128]{1,0:T(8,128)(2,1)S(1)} %fusion.1), channel_id=1, source_target_pairs={{64,0},{96,32},{0,64},{32,96},{192,128},{224,160},{128,192},{160,2... | collective-permute-start | bytes 798728 | tf_op jit(solution)/shard_map/ppermute | solution.py:104
  25.1 35.8 %collective-permute-start.3 = (bf16[1040,128]{1,0:T(8,128)(2,1)S(1)}, bf16[1040,128]{1,0:T(8,128)(2,1)S(1)}, u32[]{:S(2)}, u32[]{:S(2)}) collective-permute-start(bf16[1040,128]{1,0:T(8,128)(2,1)S(1)} %fusion.1), channel_id=1, source_target_pairs={{992,0},{64,32},{32,64},{128,96},{96,128},{192,160},{160,192},{256... | collective-permute-start | bytes 798728 | tf_op jit(solution)/shard_map/ppermute | solution.py:101
  28.7 19.2 %collective-permute-start.2 = (bf16[1040,128]{1,0:T(8,128)(2,1)S(1)}, bf16[1040,128]{1,0:T(8,128)(2,1)S(1)}, u32[]{:S(2)}, u32[]{:S(2)}) collective-permute-start(bf16[1040,128]{1,0:T(8,128)(2,1)S(1)} %fusion.1), channel_id=1, source_target_pairs={{32,0},{0,32},{96,64},{64,96},{160,128},{128,160},{224,192},{192,2... | collective-permute-start | bytes 798728 | tf_op jit(solution)/shard_map/ppermute | solution.py:104
  48.0 12.9 %collective-permute-start.4 = (bf16[1024,128]{1,0:T(8,128)(2,1)S(1)}, bf16[1024,128]{1,0:T(8,128)(2,1)S(1)}, u32[]{:S(2)}, u32[]{:S(2)}) collective-permute-start(bf16[1024,128]{1,0:T(8,128)(2,1)S(1)} %pad_maximum_fusion.4), channel_id=1, source_target_pairs={{28,0},{29,1},{30,2},{31,3},{0,4},{1,5},{2,6},{3,7},{4,8},{5,9},{6... | collective-permute-start | bytes 786440 | tf_op jit(solution)/shard_map/ppermute | solution.py:107
  51.1 9.8 %collective-permute-start.5 = (bf16[1024,128]{1,0:T(8,128)(2,1)S(1)}, bf16[1024,128]{1,0:T(8,128)(2,1)S(1)}, u32[]{:S(2)}, u32[]{:S(2)}) collective-permute-start(bf16[1024,128]{1,0:T(8,128)(2,1)S(1)} %pad_maximum_fusion.5), channel_id=1, source_target_pairs={{4,0},{5,1},{6,2},{7,3},{8,4},{9,5},{10,6},{11,7},{12,8},{13,9},{1... | collective-permute-start | bytes 786440 | tf_op jit(solution)/shard_map/ppermute | solution.py:110
  55.4 26.9 %collective-permute-start.6 = (bf16[2080,128]{1,0:T(8,128)(2,1)}, bf16[2080,128]{1,0:T(8,128)(2,1)}, u32[]{:S(2)}, u32[]{:S(2)}) collective-permute-start(bf16[2080,128]{1,0:T(8,128)(2,1)} %pad_maximum_fusion), channel_id=1, source_target_pairs={{1,0},{0,1},{3,2},{2,3},{5,4},{4,5},{7,6},{6,7},{9,8},{8,9},{11,10... | collective-permute-start | bytes 1597448 | tf_op jit(solution)/shard_map/ppermute | solution.py:113
  61.8 20.5 %collective-permute-start.7 = (bf16[2048,128]{1,0:T(8,128)(2,1)}, bf16[2048,128]{1,0:T(8,128)(2,1)}, u32[]{:S(2)}, u32[]{:S(2)}) collective-permute-start(bf16[2048,128]{1,0:T(8,128)(2,1)} %pad_maximum_fusion.2), channel_id=1, source_target_pairs={{1,0},{0,1},{3,2},{2,3},{5,4},{4,5},{7,6},{6,7},{9,8},{8,9},{11,10... | collective-permute-start | bytes 1572872 | tf_op jit(solution)/shard_map/ppermute | solution.py:114
  65.5 11.1 %collective-permute-start.8 = (bf16[1024,128]{1,0:T(8,128)(2,1)S(1)}, bf16[1024,128]{1,0:T(8,128)(2,1)S(1)}, u32[]{:S(2)}, u32[]{:S(2)}) collective-permute-start(bf16[1024,128]{1,0:T(8,128)(2,1)S(1)} %pad_maximum_fusion.6), channel_id=1, source_target_pairs={{28,0},{29,1},{30,2},{31,3},{0,4},{1,5},{2,6},{3,7},{4,8},{5,9},{6... | collective-permute-start | bytes 786440 | tf_op jit(solution)/shard_map/ppermute | solution.py:107
  68.6 15.3 %copy-start = (bf16[8,4,128,128]{3,2,1,0:T(8,128)(2,1)S(1)}, bf16[8,4,128,128]{3,2,1,0:T(8,128)(2,1)}, u32[]{:S(2)}) copy-start(bf16[8,4,128,128]{3,2,1,0:T(8,128)(2,1)} %param.5) | copy-start | bytes 3145732
  68.7 9.6 %collective-permute-start.9 = (bf16[1024,128]{1,0:T(8,128)(2,1)S(1)}, bf16[1024,128]{1,0:T(8,128)(2,1)S(1)}, u32[]{:S(2)}, u32[]{:S(2)}) collective-permute-start(bf16[1024,128]{1,0:T(8,128)(2,1)S(1)} %pad_maximum_fusion.7), channel_id=1, source_target_pairs={{4,0},{5,1},{6,2},{7,3},{8,4},{9,5},{10,6},{11,7},{12,8},{13,9},{1... | collective-permute-start | bytes 786440 | tf_op jit(solution)/shard_map/ppermute | solution.py:110
  73.1 9.2 %collective-permute-start.10 = (bf16[2080,128]{1,0:T(8,128)(2,1)}, bf16[2080,128]{1,0:T(8,128)(2,1)}, u32[]{:S(2)}, u32[]{:S(2)}) collective-permute-start(bf16[2080,128]{1,0:T(8,128)(2,1)} %pad_maximum_fusion.1), channel_id=1, source_target_pairs={{1,0},{0,1},{3,2},{2,3},{5,4},{4,5},{7,6},{6,7},{9,8},{8,9},{11,10... | collective-permute-start | bytes 1597448 | tf_op jit(solution)/shard_map/ppermute | solution.py:113
  79.1 4.9 %collective-permute-start.11 = (bf16[2048,128]{1,0:T(8,128)(2,1)}, bf16[2048,128]{1,0:T(8,128)(2,1)}, u32[]{:S(2)}, u32[]{:S(2)}) collective-permute-start(bf16[2048,128]{1,0:T(8,128)(2,1)} %pad_maximum_fusion.3), channel_id=1, source_target_pairs={{1,0},{0,1},{3,2},{2,3},{5,4},{4,5},{7,6},{6,7},{9,8},{8,9},{11,10... | collective-permute-start | bytes 1572872 | tf_op jit(solution)/shard_map/ppermute | solution.py:114

commit v3 on v2

--- a/solution.py
+++ b/solution.py
@@ -83,7 +83,7 @@
 def body(pvals, pcols, out_cols):
     row_count, slots, bs, _ = pvals.shape
     panel = row_count * slots * bs
-    quarter, eighth = panel // 4, panel // 8
+    half, quarter, eighth = panel // 2, panel // 4, panel // 8
     total_rows = row_count * lax.axis_size("blk")
     own = lax.axis_index("blk")
     place = lax.axis_index("col")
@@ -93,32 +93,43 @@
     own_cols = pcols.reshape(-1)
     tail = jnp.zeros((16, bs), jnp.bfloat16)
     tail = tail.at[0, : own_cols.shape[0]].set(own_cols.astype(jnp.bfloat16))
-    mine = lax.dynamic_slice_in_dim(flat, (2 * parity + core) * quarter, quarter, 0)
-    parcel = jnp.concatenate([mine, tail], 0)
+
+    def parcel(at, rows):
+        return jnp.concatenate([lax.dynamic_slice_in_dim(flat, at, rows, 0), tail], 0)
 
     count = lax.axis_size("blk")
+    small = parcel((2 * parity + core) * quarter, quarter)
     late = [
-        lax.ppermute(parcel, "blk", swap_routes(lambda i, d=d: (((i + d) ^ d) - d) % count))
+        lax.ppermute(small, "blk", swap_routes(lambda i, d=d: (((i + d) ^ d) - d) % count))
         for d in (1, 2)
     ]
-    early = [lax.ppermute(parcel, "blk", swap_routes(lambda i, d=d: i ^ d)) for d in (1, 2)]
-
-    def spread(arrived):
-        left = lax.ppermute(
-            jnp.concatenate([x[:eighth] for x in arrived], 0), "col", col_routes(lambda i: i - 4)
-        )
-        right = lax.ppermute(
-            jnp.concatenate([x[eighth:quarter] for x in arrived], 0), "col", col_routes(lambda i: i + 4)
-        )
-        other = lax.ppermute(jnp.concatenate(arrived, 0), "col", col_routes(lambda i: i ^ 1))
-        sides = lax.ppermute(jnp.concatenate([left, right], 0), "col", col_routes(lambda i: i ^ 1))
-        return [*arrived, left, right, other, sides]
+    large = parcel(core * half, half)
+    early = [lax.ppermute(large, "blk", swap_routes(lambda i, d=d: i ^ d)) for d in (1, 2)]
 
     def local(ids):
         return jnp.bitwise_and(ids - window_start, total_rows - 1).astype(jnp.int32)
 
+    wanted = local(out_cols[:, 0])
+    bound = REACH * row_count
+    rows = jnp.arange(row_count, dtype=jnp.int32)
+    offsets = jnp.bitwise_and(wanted - rows, total_rows - 1)
+    late, skipped = lax.optimization_barrier((late, lax.psum(offsets, "col")))
+    skipped = bound * (2 * bound + 1) - skipped + rows
+
+    def from_core(arrays):
+        return lax.ppermute(jnp.concatenate(arrays, 0), "col", col_routes(lambda i: i ^ 1))
+
+    left = lax.ppermute(
+        jnp.concatenate([x[:eighth] for x in late], 0), "col", col_routes(lambda i: i - 4)
+    )
+    right = lax.ppermute(
+        jnp.concatenate([x[eighth:quarter] for x in late], 0), "col", col_routes(lambda i: i + 4)
+    )
+    others = [from_core(early), from_core(late)]
+    sides = from_core([left, right])
+
     def listed(x):
-        return x[quarter, : own_cols.shape[0]]
+        return x[x.shape[0] - 16, : own_cols.shape[0]]
 
     odd = [jnp.bitwise_and(own, d) != 0 for d in (1, 2)]
     ahead = [jnp.where(o, listed(x), listed(y)) for o, x, y in zip(odd, late, early)]
@@ -127,31 +138,24 @@
         [behind[1], behind[0], own_cols.astype(jnp.bfloat16), ahead[0], ahead[1]]
     )
     window_cols = local(window_cols.astype(jnp.int32))
-    wanted = local(out_cols[:, 0])
-    bound = REACH * row_count
-    rows = jnp.arange(row_count, dtype=jnp.int32)
-    offsets = jnp.bitwise_and(wanted - rows, total_rows - 1)
-    skipped = bound * (2 * bound + 1) - lax.psum(offsets, "col") + rows
-
-    early_pieces = spread(early)
-    late, early_pieces[2:4] = lax.optimization_barrier((late, early_pieces[2:4]))
-    pieces = [flat] + early_pieces + spread(late)
+    pieces = [flat, *early, *late, left, right, *others, sides]
+    near, far = (
+        [(REACH + jnp.where(o, -way, way) * d) * panel for o, d in zip(odd, (1, 2))]
+        for way in (1, -1)
+    )
     site = {
         (h, c): (2 * (parity ^ h) + (core ^ c)) * quarter for h in (0, 1) for c in (0, 1)
     }
     layout, targets = [[(0, panel)]], [jnp.int32(REACH * panel)]
-    for way in (1, -1):
-        tops = [(REACH + jnp.where(o, -way, way) * d) * panel for o, d in zip(odd, (1, 2))]
-        for top in tops:
-            layout.append([(0, quarter)])
-            targets.append(top + site[0, 0])
-        for shift in (0, eighth):
-            layout.append([(0, eighth), (eighth, eighth)])
-            targets += [top + site[1, 0] + shift for top in tops]
-        layout.append([(0, quarter), (quarter + 16, quarter)])
-        targets += [top + site[0, 1] for top in tops]
-        layout.append([(j * eighth, eighth) for j in range(4)])
-        targets += [top + site[1, 1] + shift for shift in (0, eighth) for top in tops]
+    layout += [[(0, half)] for _ in near] + [[(0, quarter)] for _ in far]
+    targets += [top + core * half for top in near] + [top + site[0, 0] for top in far]
+    for shift in (0, eighth):
+        layout.append([(0, eighth), (eighth, eighth)])
+        targets += [top + site[1, 0] + shift for top in far]
+    layout += [[(0, rows), (rows + 16, rows)] for rows in (half, quarter)]
+    targets += [top + (1 - core) * half for top in near] + [top + site[0, 1] for top in far]
+    layout.append([(j * eighth, eighth) for j in range(4)])
+    targets += [top + site[1, 1] + shift for shift in (0, eighth) for top in far]
     targets = jnp.stack(targets).astype(jnp.int32)
 
     smem = pl.BlockSpec(memory_space=pltpu.SMEM)

time: 91.6 us -> 75.7 us (0.83)
  starting transfers between devices: 57.5 us -> 44.6 us
  waiting for transfers between devices: 4.46 us -> 2.05 us
    ppermute x12 -> x9, starting transfers between devices: 57.5 us -> 44.6 us  [the longest x2 24.2 us: body(): lax.ppermute(small, 'blk', swap_routes(lambda i, d=d: ((i + d ^ d) - d) %...]
    ppermute x12 -> x9, waiting for transfers between devices: 4.46 us -> 2.05 us  [the longest x3 1.72 us: from_core(): lax.ppermute(jnp.concatenate(arrays, 0), 'col', col_routes(lambda i: i ^ 1))]
    concatenate x9 -> x7, other arithmetic: 3.46 us -> 3.67 us  [the longest x3 2.77 us: from_core(): jnp.concatenate(arrays, 0)]
  transfers between devices with their start and end apart: 12 -> 9, of which waited for: 3 -> 2; matrix products, arithmetic and copies ran while one was open for 4% -> 5% of each run, Pallas kernels for 0% -> 0%
where the time goes in v3:
time: 75.7 us; the launch traced here: 75.3 us
  starting transfers between devices  44.6 us (59%)
  blocking collectives  15.8 us (21%)
  Pallas kernels  6.61 us (9%)
  other arithmetic  4.48 us (6%)
  waiting for transfers between devices  2.05 us (3%)
  local copies, waits for them, and re-layouts  1.55 us (2%)
    ppermute x2, starting transfers between devices, body(): lax.ppermute(small, 'blk', swap_routes(lambda i, d=d: ((i + d ^ d) - d) %...  24.2 us
    psum x1, blocking collectives, body(): late, skipped = lax.optimization_barrier((late, lax.psum(offsets, 'col')))  15.8 us
    ppermute x3, starting transfers between devices, from_core(): lax.ppermute(jnp.concatenate(arrays, 0), 'col', col_routes(lambda i: i ^ 1))  10.1 us
    pallas_call x1, Pallas kernels, body(): pl.pallas_call(lambda *refs: purify_kernel(layout, bs, slots, *refs), out...  6.61 us
    ppermute x2, starting transfers between devices, body(): lax.ppermute(large, 'blk', swap_routes(lambda i, d=d: i ^ d))  3.83 us
    ppermute x1, starting transfers between devices, body(): lax.ppermute(jnp.concatenate([x[eighth:quarter] for x in late], 0), 'col'...  3.37 us
    ppermute x1, starting transfers between devices, body(): lax.ppermute(jnp.concatenate([x[:eighth] for x in late], 0), 'col', col_r...  3.12 us
    concatenate x3, other arithmetic, from_core(): jnp.concatenate(arrays, 0)  2.77 us
  transfers between devices with their start and end apart: 9, of which 2 were waited for; matrix products, arithmetic and copies ran while one was open for 5% of the time, Pallas kernels for 0%

profile of v3, /device:TPU:1, one launch (start us, length us, event | category | flops | bytes accessed | tf_op | source)
XLA Modules:
  0.0 75.3 jit_solution(12735491953443822387)
XLA Ops:
  0.0 0.0 copy-start
  0.0 0.8 %convert_element_type.18 = bf16[8,4]{0,1:T(4,128)(2,1)S(1)} convert(s32[8,4]{0,1:T(4,128)} %param.6) | non-fusion elementwise | flops 32 | bytes 192 | tf_op jit(solution)/shard_map/convert_element_type | solution.py:95
  0.8 0.1 copy.6
  0.9 0.1 convert_element_type.19
  1.0 1.0 %constant_dynamic-slice_fusion = bf16[1024,128]{1,0:T(8,128)(2,1)S(1)} fusion(bf16[4096,128]{1,0:T(8,128)(2,1)} %bitcast.28, s32[]{:T(128)S(6)} %select_n.59), kind=kLoop, calls=%fused_computation.19 | loop fusion | bytes 524292 | tf_op jit(solution)/shard_map/dynamic_slice | solution.py:98
  2.0 20.6 %collective-permute-start.1 = (bf16[1040,128]{1,0:T(8,128)(2,1)S(1)}, bf16[1040,128]{1,0:T(8,128)(2,1)S(1)}, u32[]{:S(2)}, u32[]{:S(2)}) collective-permute-start(bf16[1040,128]{1,0:T(8,128)(2,1)S(1)} %pad_maximum_fusion.4), channel_id=1, source_target_pairs={{992,0},{64,32},{32,64},{128,96},{96,128},{192,160},{160,192},{256... | collective-permute-start | bytes 798728 | tf_op jit(solution)/shard_map/ppermute | solution.py:103
  22.6 3.5 %collective-permute-start.2 = (bf16[1040,128]{1,0:T(8,128)(2,1)S(1)}, bf16[1040,128]{1,0:T(8,128)(2,1)S(1)}, u32[]{:S(2)}, u32[]{:S(2)}) collective-permute-start(bf16[1040,128]{1,0:T(8,128)(2,1)S(1)} %pad_maximum_fusion.4), channel_id=1, source_target_pairs={{960,0},{992,32},{128,64},{160,96},{64,128},{96,160},{256,192},{28... | collective-permute-start | bytes 798728 | tf_op jit(solution)/shard_map/ppermute | solution.py:103
  26.2 0.0 copy-done
  26.2 0.0 copy-start.1
  26.2 0.8 %pad_maximum_fusion.2 = bf16[2064,128]{1,0:T(8,128)(2,1)} fusion(bf16[16,128]{1,0:T(8,128)(2,1)S(1)} %scatter.4, bf16[2048,128]{1,0:T(8,128)(2,1)S(1)} %constant_dynamic-slice_fusion.1), kind=kLoop, calls=%fused_computation.2 | loop fusion | flops 1056768 | bytes 1056768 | tf_op jit(solution)/shard_map/concatenate | solution.py:98
  27.1 1.9 %collective-permute-start = (bf16[2064,128]{1,0:T(8,128)(2,1)}, bf16[2064,128]{1,0:T(8,128)(2,1)S(1)}, u32[]{:S(2)}, u32[]{:S(2)}) collective-permute-start(bf16[2064,128]{1,0:T(8,128)(2,1)} %pad_maximum_fusion.2), channel_id=1, source_target_pairs={{64,0},{96,32},{0,64},{32,96},{192,128},{224,160},{128,192},{160,2... | collective-permute-start | bytes 1585160 | tf_op jit(solution)/shard_map/ppermute | solution.py:107
  29.0 1.9 %collective-permute-start.3 = (bf16[2064,128]{1,0:T(8,128)(2,1)}, bf16[2064,128]{1,0:T(8,128)(2,1)S(1)}, u32[]{:S(2)}, u32[]{:S(2)}) collective-permute-start(bf16[2064,128]{1,0:T(8,128)(2,1)} %pad_maximum_fusion.2), channel_id=1, source_target_pairs={{32,0},{0,32},{96,64},{64,96},{160,128},{128,160},{224,192},{192,2... | collective-permute-start | bytes 1585160 | tf_op jit(solution)/shard_map/ppermute | solution.py:107
  30.9 0.0 copy-done.1
  31.0 15.8 %psum.7 = s32[8]{0:T(128)S(1)} all-reduce(s32[8]{0:T(128)S(1)} %get-tuple-element.23), channel_id=1, replica_groups=mesh['blk'=32,'col'=32] {'col'}, use_global_device_ids=true, to_apply=%region_0.0 | all-reduce | flops 8 | bytes 64 | tf_op jit(solution)/shard_map/psum | solution.py:116
  46.7 0.1 convert_element_type.20
  46.8 0.1 stack.67.refs_0_
  46.9 0.0 collective-permute-done.1.refs_7_
  46.9 0.3 collective-permute-done.2.refs_8_
  47.2 0.1 fusion.4
  47.3 3.1 %collective-permute-start.4 = (bf16[1024,128]{1,0:T(8,128)(2,1)S(1)}, bf16[1024,128]{1,0:T(8,128)(2,1)S(1)}, u32[]{:S(2)}, u32[]{:S(2)}) collective-permute-start(bf16[1024,128]{1,0:T(8,128)(2,1)S(1)} %pad_maximum_fusion.5), channel_id=1, source_target_pairs={{28,0},{29,1},{30,2},{31,3},{0,4},{1,5},{2,6},{3,7},{4,8},{5,9},{6... | collective-permute-start | bytes 786440 | tf_op jit(solution)/shard_map/ppermute | solution.py:122
  50.5 3.4 %collective-permute-start.5 = (bf16[1024,128]{1,0:T(8,128)(2,1)S(1)}, bf16[1024,128]{1,0:T(8,128)(2,1)S(1)}, u32[]{:S(2)}, u32[]{:S(2)}) collective-permute-start(bf16[1024,128]{1,0:T(8,128)(2,1)S(1)} %pad_maximum_fusion.6), channel_id=1, source_target_pairs={{4,0},{5,1},{6,2},{7,3},{8,4},{9,5},{10,6},{11,7},{12,8},{13,9},{1... | collective-permute-start | bytes 786440 | tf_op jit(solution)/shard_map/ppermute | solution.py:125
  53.8 0.8 %pad_maximum_fusion.1 = bf16[2080,128]{1,0:T(8,128)(2,1)} fusion(bf16[1040,128]{1,0:T(8,128)(2,1)S(1)} %collective-permute-done.2.refs_8_, bf16[1040,128]{1,0:T(8,128)(2,1)S(1)} %collective-permute-done.1.refs_7_), kind=kLoop, calls=%fused_computation.1 | loop fusion | flops 1064960 | bytes 1064960 | tf_op jit(solution)/shard_map/concatenate | solution.py:120
  54.7 5.8 %collective-permute-start.7 = (bf16[2080,128]{1,0:T(8,128)(2,1)}, bf16[2080,128]{1,0:T(8,128)(2,1)}, u32[]{:S(2)}, u32[]{:S(2)}) collective-permute-start(bf16[2080,128]{1,0:T(8,128)(2,1)} %pad_maximum_fusion.1), channel_id=1, source_target_pairs={{1,0},{0,1},{3,2},{2,3},{5,4},{4,5},{7,6},{6,7},{9,8},{8,9},{11,10... | collective-permute-start | bytes 1597448 | tf_op jit(solution)/shard_map/ppermute | solution.py:120
  60.5 0.0 collective-permute-done.refs_6_
  60.5 0.0 collective-permute-done.3.refs_5_
  60.6 1.1 %pad_maximum_fusion = bf16[4128,128]{1,0:T(8,128)(2,1)} fusion(bf16[2064,128]{1,0:T(8,128)(2,1)S(1)} %collective-permute-done.refs_6_, bf16[2064,128]{1,0:T(8,128)(2,1)S(1)} %collective-permute-done.3.refs_5_), kind=kLoop, calls=%fused_computation | loop fusion | flops 2113536 | bytes 2113536 | tf_op jit(solution)/shard_map/concatenate | solution.py:120
  61.6 1.9 %collective-permute-start.6 = (bf16[4128,128]{1,0:T(8,128)(2,1)}, bf16[4128,128]{1,0:T(8,128)(2,1)}, u32[]{:S(2)}, u32[]{:S(2)}) collective-permute-start(bf16[4128,128]{1,0:T(8,128)(2,1)} %pad_maximum_fusion), channel_id=1, source_target_pairs={{1,0},{0,1},{3,2},{2,3},{5,4},{4,5},{7,6},{6,7},{9,8},{8,9},{11,10... | collective-permute-start | bytes 3170312 | tf_op jit(solution)/shard_map/ppermute | solution.py:120
  63.6 0.0 collective-permute-done.4.refs_9_
  63.6 0.0 collective-permute-done.5.refs_10_
  63.6 0.8 %pad_maximum_fusion.3 = bf16[2048,128]{1,0:T(8,128)(2,1)} fusion(bf16[1024,128]{1,0:T(8,128)(2,1)S(1)} %collective-permute-done.5.refs_10_, bf16[1024,128]{1,0:T(8,128)(2,1)S(1)} %collective-permute-done.4.refs_9_), kind=kLoop, calls=%fused_computation.3 | loop fusion | flops 1048576 | bytes 1048576 | tf_op jit(solution)/shard_map/concatenate | solution.py:120
  64.4 2.4 %collective-permute-start.8 = (bf16[2048,128]{1,0:T(8,128)(2,1)}, bf16[2048,128]{1,0:T(8,128)(2,1)}, u32[]{:S(2)}, u32[]{:S(2)}) collective-permute-start(bf16[2048,128]{1,0:T(8,128)(2,1)} %pad_maximum_fusion.3), channel_id=1, source_target_pairs={{1,0},{0,1},{3,2},{2,3},{5,4},{4,5},{7,6},{6,7},{9,8},{8,9},{11,10... | collective-permute-start | bytes 1572872 | tf_op jit(solution)/shard_map/ppermute | solution.py:120
  66.9 0.1 concatenate.28
  67.0 0.0 collective-permute-done.7.refs_12_
  67.0 1.7 %collective-permute-done.8.refs_13_ = bf16[2048,128]{1,0:T(8,128)(2,1)} collective-permute-done((bf16[2048,128]{1,0:T(8,128)(2,1)}, bf16[2048,128]{1,0:T(8,128)(2,1)}, u32[]{:S(2)}, u32[]{:S(2)}) %collective-permute-start.8) | collective-permute-done | bytes 524320 | tf_op jit(solution)/shard_map/ppermute | solution.py:120
  68.7 0.0 collective-permute-done.6.refs_11_
  68.7 6.6 %purify.1 = bf16[8,1,128,128]{3,2,1,0:T(8,128)(2,1)} custom-call(s32[17]{0:T(128)S(1)} %stack.67.refs_0_, s32[160]{0:T(256)S(1)} %subtract_and_fusion.refs_1_, s32[8]{0:T(128)S(1)} %get-tuple-element.24.refs_2_, s32[8]{0:T(128)S(1)} %iota_add_fusion.refs_3_, bf16[4096,128]{1,0:T(8,128)(2,1)S(1)} %bitcast.30, ...), custom_call_target="tpu_custom_call" | custom-call | tf_op jit(solution)/shard_map/purify/pallas_call | solution.py:163
  (10 shorter events, 0.1 us)
Async XLA Ops:
  0.0 26.2 %copy-start = (bf16[8,4,128,128]{3,2,1,0:T(8,128)(2,1)S(1)}, bf16[8,4,128,128]{3,2,1,0:T(8,128)(2,1)}, u32[]{:S(2)}) copy-start(bf16[8,4,128,128]{3,2,1,0:T(8,128)(2,1)} %param.5) | copy-start | bytes 3145732
  2.0 44.9 %collective-permute-start.1 = (bf16[1040,128]{1,0:T(8,128)(2,1)S(1)}, bf16[1040,128]{1,0:T(8,128)(2,1)S(1)}, u32[]{:S(2)}, u32[]{:S(2)}) collective-permute-start(bf16[1040,128]{1,0:T(8,128)(2,1)S(1)} %pad_maximum_fusion.4), channel_id=1, source_target_pairs={{992,0},{64,32},{32,64},{128,96},{96,128},{192,160},{160,192},{256... | collective-permute-start | bytes 798728 | tf_op jit(solution)/shard_map/ppermute | solution.py:103
  22.6 24.6 %collective-permute-start.2 = (bf16[1040,128]{1,0:T(8,128)(2,1)S(1)}, bf16[1040,128]{1,0:T(8,128)(2,1)S(1)}, u32[]{:S(2)}, u32[]{:S(2)}) collective-permute-start(bf16[1040,128]{1,0:T(8,128)(2,1)S(1)} %pad_maximum_fusion.4), channel_id=1, source_target_pairs={{960,0},{992,32},{128,64},{160,96},{64,128},{96,160},{256,192},{28... | collective-permute-start | bytes 798728 | tf_op jit(solution)/shard_map/ppermute | solution.py:103
  26.2 4.8 %copy-start.1 = (s32[8,1]{0,1:T(1,128)S(1)}, s32[8,1]{0,1:T(1,128)}, u32[]{:S(2)}) copy-start(s32[8,1]{0,1:T(1,128)} %param.7) | copy-start | bytes 100
  27.1 33.4 %collective-permute-start = (bf16[2064,128]{1,0:T(8,128)(2,1)}, bf16[2064,128]{1,0:T(8,128)(2,1)S(1)}, u32[]{:S(2)}, u32[]{:S(2)}) collective-permute-start(bf16[2064,128]{1,0:T(8,128)(2,1)} %pad_maximum_fusion.2), channel_id=1, source_target_pairs={{64,0},{96,32},{0,64},{32,96},{192,128},{224,160},{128,192},{160,2... | collective-permute-start | bytes 1585160 | tf_op jit(solution)/shard_map/ppermute | solution.py:107
  29.0 31.5 %collective-permute-start.3 = (bf16[2064,128]{1,0:T(8,128)(2,1)}, bf16[2064,128]{1,0:T(8,128)(2,1)S(1)}, u32[]{:S(2)}, u32[]{:S(2)}) collective-permute-start(bf16[2064,128]{1,0:T(8,128)(2,1)} %pad_maximum_fusion.2), channel_id=1, source_target_pairs={{32,0},{0,32},{96,64},{64,96},{160,128},{128,160},{224,192},{192,2... | collective-permute-start | bytes 1585160 | tf_op jit(solution)/shard_map/ppermute | solution.py:107
  47.3 16.2 %collective-permute-start.4 = (bf16[1024,128]{1,0:T(8,128)(2,1)S(1)}, bf16[1024,128]{1,0:T(8,128)(2,1)S(1)}, u32[]{:S(2)}, u32[]{:S(2)}) collective-permute-start(bf16[1024,128]{1,0:T(8,128)(2,1)S(1)} %pad_maximum_fusion.5), channel_id=1, source_target_pairs={{28,0},{29,1},{30,2},{31,3},{0,4},{1,5},{2,6},{3,7},{4,8},{5,9},{6... | collective-permute-start | bytes 786440 | tf_op jit(solution)/shard_map/ppermute | solution.py:122
  50.5 13.1 %collective-permute-start.5 = (bf16[1024,128]{1,0:T(8,128)(2,1)S(1)}, bf16[1024,128]{1,0:T(8,128)(2,1)S(1)}, u32[]{:S(2)}, u32[]{:S(2)}) collective-permute-start(bf16[1024,128]{1,0:T(8,128)(2,1)S(1)} %pad_maximum_fusion.6), channel_id=1, source_target_pairs={{4,0},{5,1},{6,2},{7,3},{8,4},{9,5},{10,6},{11,7},{12,8},{13,9},{1... | collective-permute-start | bytes 786440 | tf_op jit(solution)/shard_map/ppermute | solution.py:125
  54.7 12.3 %collective-permute-start.7 = (bf16[2080,128]{1,0:T(8,128)(2,1)}, bf16[2080,128]{1,0:T(8,128)(2,1)}, u32[]{:S(2)}, u32[]{:S(2)}) collective-permute-start(bf16[2080,128]{1,0:T(8,128)(2,1)} %pad_maximum_fusion.1), channel_id=1, source_target_pairs={{1,0},{0,1},{3,2},{2,3},{5,4},{4,5},{7,6},{6,7},{9,8},{8,9},{11,10... | collective-permute-start | bytes 1597448 | tf_op jit(solution)/shard_map/ppermute | solution.py:120
  61.6 7.1 %collective-permute-start.6 = (bf16[4128,128]{1,0:T(8,128)(2,1)}, bf16[4128,128]{1,0:T(8,128)(2,1)}, u32[]{:S(2)}, u32[]{:S(2)}) collective-permute-start(bf16[4128,128]{1,0:T(8,128)(2,1)} %pad_maximum_fusion), channel_id=1, source_target_pairs={{1,0},{0,1},{3,2},{2,3},{5,4},{4,5},{7,6},{6,7},{9,8},{8,9},{11,10... | collective-permute-start | bytes 3170312 | tf_op jit(solution)/shard_map/ppermute | solution.py:120
  64.4 4.3 %collective-permute-start.8 = (bf16[2048,128]{1,0:T(8,128)(2,1)}, bf16[2048,128]{1,0:T(8,128)(2,1)}, u32[]{:S(2)}, u32[]{:S(2)}) collective-permute-start(bf16[2048,128]{1,0:T(8,128)(2,1)} %pad_maximum_fusion.3), channel_id=1, source_target_pairs={{1,0},{0,1},{3,2},{2,3},{5,4},{4,5},{7,6},{6,7},{9,8},{8,9},{11,10... | collective-permute-start | bytes 1572872 | tf_op jit(solution)/shard_map/ppermute | solution.py:120

commit v4 on v3

--- a/solution.py
+++ b/solution.py
@@ -15,42 +15,16 @@
 
 
 def purify_kernel(layout, bs, slots, targets_ref, cols_ref, wanted_ref, skipped_ref, *refs):
-    pieces, out_ref, window, picks, sems = refs[:-4], refs[-4], refs[-3], refs[-2], refs[-1]
+    pieces, out_ref, window = refs[:-2], refs[-2], refs[-1]
     row_count = out_ref.shape[0]
     nothing = window.shape[0] // bs - 1
-    copies = []
-    for ref, moves in zip(pieces, layout, strict=True):
-        for source, rows in moves:
-            start = pl.multiple_of(targets_ref[len(copies)], bs)
-            copies.append(
-                pltpu.make_async_copy(
-                    ref.at[pl.ds(source, rows)],
-                    window.at[pl.ds(start, rows)],
-                    sems.at[len(copies)],
-                )
-            )
-            copies[-1].start()
-    window[pl.ds(nothing * bs, bs)] = jnp.zeros((bs, window.shape[1]), window.dtype)
-
     first = REACH * row_count
 
-    def find_row(r, carry):
-        column, skipped = wanted_ref[r], skipped_ref[r]
-        for a in range(slots):
-            base = cols_ref[(first + r) * slots + a] * slots
-            for b in range(slots):
-                q = cols_ref[base + b]
-                found = jnp.int32(nothing)
-                for m in range(slots):
-                    found = jnp.where(cols_ref[q * slots + m] == column, q * slots + m, found)
-                found = jnp.where(q == skipped, nothing, found)
-                picks[r * 32 + a * slots + b] = found
-                picks[r * 32 + 16 + a * slots + b] = jnp.where(q == column, base + b, nothing)
-        return carry
-
-    lax.fori_loop(0, row_count, find_row, 0)
-    for copy in copies:
-        copy.wait()
+    moves = [(ref, *move) for ref, given in zip(pieces, layout, strict=True) for move in given]
+    for i, (ref, source, rows) in enumerate(moves):
+        start = pl.multiple_of(targets_ref[i], bs)
+        window[pl.ds(start, rows)] = ref[pl.ds(source, rows)]
+    window[pl.ds(nothing * bs, bs)] = jnp.zeros((bs, window.shape[1]), window.dtype)
 
     def block(index):
         return window[pl.ds(pl.multiple_of(index * bs, bs), bs)]
@@ -59,17 +33,28 @@
         return jnp.concatenate([block(i) for i in indices], axis=axis)
 
     for r in range(row_count):
+        column, skipped = wanted_ref[r], skipped_ref[r]
         direct, high, low = [], [], []
         for a in range(slots):
             base = cols_ref[(first + r) * slots + a] * slots
-            left = stack([base + b for b in range(slots)], 1)
-            right = stack([picks[r * 32 + a * slots + b] for b in range(slots)], 0)
-            total = jnp.dot(left, right, preferred_element_type=jnp.float32)
+            reached, hit = [], jnp.int32(nothing)
+            for b in range(slots):
+                q = cols_ref[base + b]
+                found = jnp.int32(nothing)
+                for m in range(slots):
+                    here = q * slots + m
+                    found = jnp.where(cols_ref[here] == column, here, found)
+                reached.append(jnp.where(q == skipped, nothing, found))
+                hit = jnp.where(q == column, base + b, hit)
+            total = jnp.dot(
+                stack([base + b for b in range(slots)], 1),
+                stack(reached, 0),
+                preferred_element_type=jnp.float32,
+            )
             top = total.astype(jnp.bfloat16)
             high.append(top)
             low.append((total - top.astype(jnp.float32)).astype(jnp.bfloat16))
-            one = [block(picks[r * 32 + 16 + a * slots + b]) for b in range(slots)]
-            direct.append((one[0] + one[1]) + (one[2] + one[3]))
+            direct.append(block(hit))
         left = stack([(first + r) * slots + a for a in range(slots)], 1)
         right = jnp.concatenate(
             [jnp.concatenate(part, 0) for part in (direct, high, low)], 1
@@ -119,14 +104,13 @@
     def from_core(arrays):
         return lax.ppermute(jnp.concatenate(arrays, 0), "col", col_routes(lambda i: i ^ 1))
 
-    left = lax.ppermute(
-        jnp.concatenate([x[:eighth] for x in late], 0), "col", col_routes(lambda i: i - 4)
-    )
-    right = lax.ppermute(
-        jnp.concatenate([x[eighth:quarter] for x in late], 0), "col", col_routes(lambda i: i + 4)
-    )
-    others = [from_core(early), from_core(late)]
-    sides = from_core([left, right])
+    first = jnp.concatenate([x[:eighth] for x in late], 0)
+    second = jnp.concatenate([x[eighth:quarter] for x in late], 0)
+    (first, second), early = lax.optimization_barrier(((first, second), early))
+    left = lax.ppermute(first, "col", col_routes(lambda i: i - 4))
+    right = lax.ppermute(second, "col", col_routes(lambda i: i + 4))
+    other = from_core(early)
+    sides = from_core([left, right, *late])
 
     def listed(x):
         return x[x.shape[0] - 16, : own_cols.shape[0]]
@@ -138,7 +122,7 @@
         [behind[1], behind[0], own_cols.astype(jnp.bfloat16), ahead[0], ahead[1]]
     )
     window_cols = local(window_cols.astype(jnp.int32))
-    pieces = [flat, *early, *late, left, right, *others, sides]
+    pieces = [flat, *early, *late, left, right, other, sides]
     near, far = (
         [(REACH + jnp.where(o, -way, way) * d) * panel for o, d in zip(odd, (1, 2))]
         for way in (1, -1)
@@ -152,10 +136,12 @@
     for shift in (0, eighth):
         layout.append([(0, eighth), (eighth, eighth)])
         targets += [top + site[1, 0] + shift for top in far]
-    layout += [[(0, rows), (rows + 16, rows)] for rows in (half, quarter)]
-    targets += [top + (1 - core) * half for top in near] + [top + site[0, 1] for top in far]
+    layout.append([(0, half), (half + 16, half)])
+    targets += [top + (1 - core) * half for top in near]
     layout.append([(j * eighth, eighth) for j in range(4)])
+    layout[-1] += [(2 * quarter + j * (quarter + 16), quarter) for j in range(2)]
     targets += [top + site[1, 1] + shift for shift in (0, eighth) for top in far]
+    targets += [top + site[0, 1] for top in far]
     targets = jnp.stack(targets).astype(jnp.int32)
 
     smem = pl.BlockSpec(memory_space=pltpu.SMEM)
@@ -163,14 +149,12 @@
     return pl.pallas_call(
         lambda *refs: purify_kernel(layout, bs, slots, *refs),
         out_shape=jax.ShapeDtypeStruct((row_count, 1, bs, bs), jnp.bfloat16),
-        in_specs=[smem] * 4 + [pl.BlockSpec(memory_space=pl.ANY)] * len(pieces),
+        in_specs=[smem] * 4 + [pl.BlockSpec(memory_space=pltpu.VMEM)] * len(pieces),
         out_specs=pl.BlockSpec(memory_space=pltpu.VMEM),
         scratch_shapes=[
             pltpu.VMEM((window_rows + bs, bs), jnp.bfloat16),
-            pltpu.SMEM((row_count * 32,), jnp.int32),
-            pltpu.SemaphoreType.DMA((sum(map(len, layout)),)),
         ],
-        compiler_params=pltpu.CompilerParams(vmem_limit_bytes=10 * 2**20),
+        compiler_params=pltpu.CompilerParams(vmem_limit_bytes=16 * 2**20),
         name="purify",
     )(targets, window_cols, wanted, skipped, *pieces)
 

time: 75.7 us -> 81.7 us (1.079)
  the two profiles are of different devices: /device:TPU:1 before, /device:TPU:7 now
where the time goes in v4:
time: 81.7 us; the launch traced here: 81.3 us
  starting transfers between devices  43.2 us (53%)
  blocking collectives  15.6 us (19%)
  waiting for transfers between devices  12.4 us (15%)
  Pallas kernels  5.41 us (7%)
  other arithmetic  3.05 us (4%)
  local copies, waits for them, and re-layouts  1.54 us (2%)
    ppermute x2, starting transfers between devices, body(): lax.ppermute(small, 'blk', swap_routes(lambda i, d=d: ((i + d ^ d) - d) %...  22.4 us
    psum x1, blocking collectives, body(): late, skipped = lax.optimization_barrier((late, lax.psum(offsets, 'col')))  15.6 us
    ppermute x2, starting transfers between devices, from_core(): lax.ppermute(jnp.concatenate(arrays, 0), 'col', col_routes(lambda i: i ^ 1))  9.01 us
    ppermute x2, waiting for transfers between devices, body(): lax.ppermute(large, 'blk', swap_routes(lambda i, d=d: i ^ d))  8.41 us
    ppermute x2, starting transfers between devices, body(): lax.ppermute(large, 'blk', swap_routes(lambda i, d=d: i ^ d))  5.51 us
    pallas_call x1, Pallas kernels, body(): pl.pallas_call(lambda *refs: purify_kernel(layout, bs, slots, *refs), out...  5.41 us
    ppermute x1, starting transfers between devices, body(): left = lax.ppermute(first, 'col', col_routes(lambda i: i - 4))  4.32 us
    ppermute x2, waiting for transfers between devices, from_core(): lax.ppermute(jnp.concatenate(arrays, 0), 'col', col_routes(lambda i: i ^ 1))  2.24 us
  transfers between devices with their start and end apart: 8, of which 3 were waited for; matrix products, arithmetic and copies ran while one was open for 3% of the time, Pallas kernels for 0%

profile of v4, /device:TPU:7, one launch (start us, length us, event | category | flops | bytes accessed | tf_op | source)
XLA Modules:
  0.0 81.3 jit_solution(7268216274425965408)
XLA Ops:
  0.0 0.0 copy-start
  0.0 0.8 convert_element_type.18
  0.8 0.1 copy.6
  0.9 0.1 convert_element_type.19
  1.0 1.0 %constant_dynamic-slice_fusion.1 = bf16[1024,128]{1,0:T(8,128)(2,1)S(1)} fusion(bf16[4096,128]{1,0:T(8,128)(2,1)} %bitcast.28, s32[]{:T(128)S(6)} %select_n.58), kind=kLoop, calls=%fused_computation.19 | loop fusion | bytes 524292 | tf_op jit(solution)/shard_map/dynamic_slice | solution.py:83
  2.0 20.5 %collective-permute-start.1 = (bf16[1040,128]{1,0:T(8,128)(2,1)S(1)}, bf16[1040,128]{1,0:T(8,128)(2,1)S(1)}, u32[]{:S(2)}, u32[]{:S(2)}) collective-permute-start(bf16[1040,128]{1,0:T(8,128)(2,1)S(1)} %pad_maximum_fusion.3), channel_id=1, source_target_pairs={{960,0},{992,32},{128,64},{160,96},{64,128},{96,160},{256,192},{28... | collective-permute-start | bytes 798728 | tf_op jit(solution)/shard_map/ppermute | solution.py:88
  22.5 1.9 %collective-permute-start = (bf16[1040,128]{1,0:T(8,128)(2,1)S(1)}, bf16[1040,128]{1,0:T(8,128)(2,1)S(1)}, u32[]{:S(2)}, u32[]{:S(2)}) collective-permute-start(bf16[1040,128]{1,0:T(8,128)(2,1)S(1)} %pad_maximum_fusion.3), channel_id=1, source_target_pairs={{992,0},{64,32},{32,64},{128,96},{96,128},{192,160},{160,192},{256... | collective-permute-start | bytes 798728 | tf_op jit(solution)/shard_map/ppermute | solution.py:88
  24.4 0.0 copy-done
  24.4 0.0 copy-start.1
  24.5 3.6 %collective-permute-start.3 = (bf16[2064,128]{1,0:T(8,128)(2,1)S(1)}, bf16[2064,128]{1,0:T(8,128)(2,1)S(1)}, u32[]{:S(2)}, u32[]{:S(2)}) collective-permute-start(bf16[2064,128]{1,0:T(8,128)(2,1)S(1)} %pad_maximum_fusion.2), channel_id=1, source_target_pairs={{64,0},{96,32},{0,64},{32,96},{192,128},{224,160},{128,192},{160,2... | collective-permute-start | bytes 1585160 | tf_op jit(solution)/shard_map/ppermute | solution.py:92
  28.1 1.9 %collective-permute-start.2 = (bf16[2064,128]{1,0:T(8,128)(2,1)S(1)}, bf16[2064,128]{1,0:T(8,128)(2,1)S(1)}, u32[]{:S(2)}, u32[]{:S(2)}) collective-permute-start(bf16[2064,128]{1,0:T(8,128)(2,1)S(1)} %pad_maximum_fusion.2), channel_id=1, source_target_pairs={{32,0},{0,32},{96,64},{64,96},{160,128},{128,160},{224,192},{192,2... | collective-permute-start | bytes 1585160 | tf_op jit(solution)/shard_map/ppermute | solution.py:92
  30.1 0.0 copy-done.1
  30.1 15.6 %psum.7 = s32[8]{0:T(128)S(1)} all-reduce(s32[8]{0:T(128)S(1)} %get-tuple-element.31), channel_id=1, replica_groups=mesh['blk'=32,'col'=32] {'col'}, use_global_device_ids=true, to_apply=%region_0.0 | all-reduce | flops 8 | bytes 64 | tf_op jit(solution)/shard_map/psum | solution.py:101
  45.7 0.0 collective-permute-done.1.refs_8_
  45.7 0.0 collective-permute-done.refs_7_
  45.8 8.4 %collective-permute-done.3.refs_6_ = bf16[2064,128]{1,0:T(8,128)(2,1)S(1)} collective-permute-done((bf16[2064,128]{1,0:T(8,128)(2,1)S(1)}, bf16[2064,128]{1,0:T(8,128)(2,1)S(1)}, u32[]{:S(2)}, u32[]{:S(2)}) %collective-permute-start.3) | collective-permute-done | bytes 528416 | tf_op jit(solution)/shard_map/ppermute | solution.py:92
  54.2 0.0 collective-permute-done.2.refs_5_
  54.2 4.3 %collective-permute-start.4 = (bf16[1024,128]{1,0:T(8,128)(2,1)S(1)}, bf16[1024,128]{1,0:T(8,128)(2,1)S(1)}, u32[]{:S(2)}, u32[]{:S(2)}) collective-permute-start(bf16[1024,128]{1,0:T(8,128)(2,1)S(1)} %pad_maximum_fusion.4), channel_id=1, source_target_pairs={{28,0},{29,1},{30,2},{31,3},{0,4},{1,5},{2,6},{3,7},{4,8},{5,9},{6... | collective-permute-start | bytes 786440 | tf_op jit(solution)/shard_map/ppermute | solution.py:110
  58.5 1.9 %collective-permute-start.5 = (bf16[1024,128]{1,0:T(8,128)(2,1)S(1)}, bf16[1024,128]{1,0:T(8,128)(2,1)S(1)}, u32[]{:S(2)}, u32[]{:S(2)}) collective-permute-start(bf16[1024,128]{1,0:T(8,128)(2,1)S(1)} %pad_maximum_fusion.5), channel_id=1, source_target_pairs={{4,0},{5,1},{6,2},{7,3},{8,4},{9,5},{10,6},{11,7},{12,8},{13,9},{1... | collective-permute-start | bytes 786440 | tf_op jit(solution)/shard_map/ppermute | solution.py:111
  60.4 1.1 %pad_maximum_fusion = bf16[4128,128]{1,0:T(8,128)(2,1)} fusion(bf16[2064,128]{1,0:T(8,128)(2,1)S(1)} %collective-permute-done.3.refs_6_, bf16[2064,128]{1,0:T(8,128)(2,1)S(1)} %collective-permute-done.2.refs_5_), kind=kLoop, calls=%fused_computation | loop fusion | flops 2113536 | bytes 2113536 | tf_op jit(solution)/shard_map/concatenate | solution.py:105
  61.5 4.0 %collective-permute-start.6 = (bf16[4128,128]{1,0:T(8,128)(2,1)}, bf16[4128,128]{1,0:T(8,128)(2,1)}, u32[]{:S(2)}, u32[]{:S(2)}) collective-permute-start(bf16[4128,128]{1,0:T(8,128)(2,1)} %pad_maximum_fusion), channel_id=1, source_target_pairs={{1,0},{0,1},{3,2},{2,3},{5,4},{4,5},{7,6},{6,7},{9,8},{8,9},{11,10... | collective-permute-start | bytes 3170312 | tf_op jit(solution)/shard_map/ppermute | solution.py:105
  65.6 0.0 collective-permute-done.4.refs_9_
  65.6 1.7 %collective-permute-done.5.refs_10_ = bf16[1024,128]{1,0:T(8,128)(2,1)S(1)} collective-permute-done((bf16[1024,128]{1,0:T(8,128)(2,1)S(1)}, bf16[1024,128]{1,0:T(8,128)(2,1)S(1)}, u32[]{:S(2)}, u32[]{:S(2)}) %collective-permute-start.5) | collective-permute-done | bytes 262176 | tf_op jit(solution)/shard_map/ppermute | solution.py:111
  67.3 1.1 %pad_maximum_fusion.1 = bf16[4128,128]{1,0:T(8,128)(2,1)} fusion(bf16[1040,128]{1,0:T(8,128)(2,1)S(1)} %collective-permute-done.1.refs_8_, bf16[1040,128]{1,0:T(8,128)(2,1)S(1)} %collective-permute-done.refs_7_, bf16[1024,128]{1,0:T(8,128)(2,1)S(1)} %collective-permute-done.5.refs_10_, bf16[1024,128]{1,0:T(8,128)(2,1)S(1)} %collective-permute-done.4.refs_9_), kind=kLoop, calls=%fused_computation.1 | loop fusion | flops 4227072 | bytes 2113536 | tf_op jit(solution)/shard_map/concatenate | solution.py:105
  68.3 5.0 %collective-permute-start.7 = (bf16[4128,128]{1,0:T(8,128)(2,1)}, bf16[4128,128]{1,0:T(8,128)(2,1)}, u32[]{:S(2)}, u32[]{:S(2)}) collective-permute-start(bf16[4128,128]{1,0:T(8,128)(2,1)} %pad_maximum_fusion.1), channel_id=1, source_target_pairs={{1,0},{0,1},{3,2},{2,3},{5,4},{4,5},{7,6},{6,7},{9,8},{8,9},{11,10... | collective-permute-start | bytes 3170312 | tf_op jit(solution)/shard_map/ppermute | solution.py:105
  73.4 0.1 convert_element_type.20
  73.5 0.1 stack.67.refs_0_
  73.6 0.1 concatenate.27
  73.7 0.0 collective-permute-done.6.refs_11_
  73.7 2.2 %collective-permute-done.7.refs_12_ = bf16[4128,128]{1,0:T(8,128)(2,1)} collective-permute-done((bf16[4128,128]{1,0:T(8,128)(2,1)}, bf16[4128,128]{1,0:T(8,128)(2,1)}, u32[]{:S(2)}, u32[]{:S(2)}) %collective-permute-start.7) | collective-permute-done | bytes 1056800 | tf_op jit(solution)/shard_map/ppermute | solution.py:105
  75.9 5.4 %purify.1 = bf16[8,1,128,128]{3,2,1,0:T(8,128)(2,1)} custom-call(s32[17]{0:T(128)S(1)} %stack.67.refs_0_, s32[160]{0:T(256)S(1)} %subtract_and_fusion.refs_1_, s32[8]{0:T(128)S(1)} %get-tuple-element.32.refs_2_, s32[8]{0:T(128)S(1)} %iota_add_fusion.refs_3_, bf16[4096,128]{1,0:T(8,128)(2,1)S(1)} %bitcast.30, ...), custom_call_target="tpu_custom_call" | custom-call | tf_op jit(solution)/shard_map/purify/pallas_call | solution.py:149
  (12 shorter events, 0.2 us)
Async XLA Ops:
  0.0 24.4 %copy-start = (bf16[8,4,128,128]{3,2,1,0:T(8,128)(2,1)S(1)}, bf16[8,4,128,128]{3,2,1,0:T(8,128)(2,1)}, u32[]{:S(2)}) copy-start(bf16[8,4,128,128]{3,2,1,0:T(8,128)(2,1)} %param.5) | copy-start | bytes 3145732
  2.0 43.7 %collective-permute-start.1 = (bf16[1040,128]{1,0:T(8,128)(2,1)S(1)}, bf16[1040,128]{1,0:T(8,128)(2,1)S(1)}, u32[]{:S(2)}, u32[]{:S(2)}) collective-permute-start(bf16[1040,128]{1,0:T(8,128)(2,1)S(1)} %pad_maximum_fusion.3), channel_id=1, source_target_pairs={{960,0},{992,32},{128,64},{160,96},{64,128},{96,160},{256,192},{28... | collective-permute-start | bytes 798728 | tf_op jit(solution)/shard_map/ppermute | solution.py:88
  22.5 23.2 %collective-permute-start = (bf16[1040,128]{1,0:T(8,128)(2,1)S(1)}, bf16[1040,128]{1,0:T(8,128)(2,1)S(1)}, u32[]{:S(2)}, u32[]{:S(2)}) collective-permute-start(bf16[1040,128]{1,0:T(8,128)(2,1)S(1)} %pad_maximum_fusion.3), channel_id=1, source_target_pairs={{992,0},{64,32},{32,64},{128,96},{96,128},{192,160},{160,192},{256... | collective-permute-start | bytes 798728 | tf_op jit(solution)/shard_map/ppermute | solution.py:88
  24.4 5.6 %copy-start.1 = (s32[8,1]{0,1:T(1,128)S(1)}, s32[8,1]{0,1:T(1,128)}, u32[]{:S(2)}) copy-start(s32[8,1]{0,1:T(1,128)} %param.7) | copy-start | bytes 100
  24.5 29.7 %collective-permute-start.3 = (bf16[2064,128]{1,0:T(8,128)(2,1)S(1)}, bf16[2064,128]{1,0:T(8,128)(2,1)S(1)}, u32[]{:S(2)}, u32[]{:S(2)}) collective-permute-start(bf16[2064,128]{1,0:T(8,128)(2,1)S(1)} %pad_maximum_fusion.2), channel_id=1, source_target_pairs={{64,0},{96,32},{0,64},{32,96},{192,128},{224,160},{128,192},{160,2... | collective-permute-start | bytes 1585160 | tf_op jit(solution)/shard_map/ppermute | solution.py:92
  28.1 26.1 %collective-permute-start.2 = (bf16[2064,128]{1,0:T(8,128)(2,1)S(1)}, bf16[2064,128]{1,0:T(8,128)(2,1)S(1)}, u32[]{:S(2)}, u32[]{:S(2)}) collective-permute-start(bf16[2064,128]{1,0:T(8,128)(2,1)S(1)} %pad_maximum_fusion.2), channel_id=1, source_target_pairs={{32,0},{0,32},{96,64},{64,96},{160,128},{128,160},{224,192},{192,2... | collective-permute-start | bytes 1585160 | tf_op jit(solution)/shard_map/ppermute | solution.py:92
  54.2 11.4 %collective-permute-start.4 = (bf16[1024,128]{1,0:T(8,128)(2,1)S(1)}, bf16[1024,128]{1,0:T(8,128)(2,1)S(1)}, u32[]{:S(2)}, u32[]{:S(2)}) collective-permute-start(bf16[1024,128]{1,0:T(8,128)(2,1)S(1)} %pad_maximum_fusion.4), channel_id=1, source_target_pairs={{28,0},{29,1},{30,2},{31,3},{0,4},{1,5},{2,6},{3,7},{4,8},{5,9},{6... | collective-permute-start | bytes 786440 | tf_op jit(solution)/shard_map/ppermute | solution.py:110
  58.5 8.8 %collective-permute-start.5 = (bf16[1024,128]{1,0:T(8,128)(2,1)S(1)}, bf16[1024,128]{1,0:T(8,128)(2,1)S(1)}, u32[]{:S(2)}, u32[]{:S(2)}) collective-permute-start(bf16[1024,128]{1,0:T(8,128)(2,1)S(1)} %pad_maximum_fusion.5), channel_id=1, source_target_pairs={{4,0},{5,1},{6,2},{7,3},{8,4},{9,5},{10,6},{11,7},{12,8},{13,9},{1... | collective-permute-start | bytes 786440 | tf_op jit(solution)/shard_map/ppermute | solution.py:111
  61.5 12.2 %collective-permute-start.6 = (bf16[4128,128]{1,0:T(8,128)(2,1)}, bf16[4128,128]{1,0:T(8,128)(2,1)}, u32[]{:S(2)}, u32[]{:S(2)}) collective-permute-start(bf16[4128,128]{1,0:T(8,128)(2,1)} %pad_maximum_fusion), channel_id=1, source_target_pairs={{1,0},{0,1},{3,2},{2,3},{5,4},{4,5},{7,6},{6,7},{9,8},{8,9},{11,10... | collective-permute-start | bytes 3170312 | tf_op jit(solution)/shard_map/ppermute | solution.py:105
  68.3 7.6 %collective-permute-start.7 = (bf16[4128,128]{1,0:T(8,128)(2,1)}, bf16[4128,128]{1,0:T(8,128)(2,1)}, u32[]{:S(2)}, u32[]{:S(2)}) collective-permute-start(bf16[4128,128]{1,0:T(8,128)(2,1)} %pad_maximum_fusion.1), channel_id=1, source_target_pairs={{1,0},{0,1},{3,2},{2,3},{5,4},{4,5},{7,6},{6,7},{9,8},{8,9},{11,10... | collective-permute-start | bytes 3170312 | tf_op jit(solution)/shard_map/ppermute | solution.py:105

commit v5 on v4

--- a/solution.py
+++ b/solution.py
@@ -106,10 +106,11 @@
 
     first = jnp.concatenate([x[:eighth] for x in late], 0)
     second = jnp.concatenate([x[eighth:quarter] for x in late], 0)
-    (first, second), early = lax.optimization_barrier(((first, second), early))
     left = lax.ppermute(first, "col", col_routes(lambda i: i - 4))
     right = lax.ppermute(second, "col", col_routes(lambda i: i + 4))
+    early = lax.optimization_barrier((early, left, second))[0]
     other = from_core(early)
+    right = lax.optimization_barrier((right, early))[0]
     sides = from_core([left, right, *late])
 
     def listed(x):

time: 81.7 us -> 75.9 us (0.929)
  the two profiles are of different devices: /device:TPU:7 before, /device:TPU:1 now
where the time goes in v5:
time: 75.9 us; the launch traced here: 75.5 us
  starting transfers between devices  43.2 us (57%)
  blocking collectives  15.7 us (21%)
  waiting for transfers between devices  5.5 us (7%)
  Pallas kernels  5.41 us (7%)
  other arithmetic  3.84 us (5%)
  local copies, waits for them, and re-layouts  1.54 us (2%)
    ppermute x2, starting transfers between devices, body(): lax.ppermute(small, 'blk', swap_routes(lambda i, d=d: ((i + d ^ d) - d) %...  23.2 us
    psum x1, blocking collectives, body(): late, skipped = lax.optimization_barrier((late, lax.psum(offsets, 'col')))  15.7 us
    ppermute x2, starting transfers between devices, from_core(): lax.ppermute(jnp.concatenate(arrays, 0), 'col', col_routes(lambda i: i ^ 1))  8.02 us
    ppermute x2, starting transfers between devices, body(): lax.ppermute(large, 'blk', swap_routes(lambda i, d=d: i ^ d))  5.5 us
    pallas_call x1, Pallas kernels, body(): pl.pallas_call(lambda *refs: purify_kernel(layout, bs, slots, *refs), out...  5.41 us
    ppermute x1, starting transfers between devices, body(): right = lax.ppermute(second, 'col', col_routes(lambda i: i + 4))  3.43 us
    ppermute x1, starting transfers between devices, body(): left = lax.ppermute(first, 'col', col_routes(lambda i: i - 4))  3.06 us
    ppermute x2, waiting for transfers between devices, from_core(): lax.ppermute(jnp.concatenate(arrays, 0), 'col', col_routes(lambda i: i ^ 1))  2.6 us
  transfers between devices with their start and end apart: 8, of which 3 were waited for; matrix products, arithmetic and copies ran while one was open for 5% of the time, Pallas kernels for 0%

profile of v5, /device:TPU:1, one launch (start us, length us, event | category | flops | bytes accessed | tf_op | source)
XLA Modules:
  0.0 75.5 jit_solution(1808011960634026956)
XLA Ops:
  0.0 0.0 copy-start
  0.0 0.8 %convert_element_type.18 = bf16[8,4]{0,1:T(4,128)(2,1)S(1)} convert(s32[8,4]{0,1:T(4,128)} %param.6) | non-fusion elementwise | flops 32 | bytes 192 | tf_op jit(solution)/shard_map/convert_element_type | solution.py:80
  0.8 0.1 copy.6
  0.9 0.1 convert_element_type.19
  1.0 1.0 %constant_dynamic-slice_fusion = bf16[1024,128]{1,0:T(8,128)(2,1)S(1)} fusion(bf16[4096,128]{1,0:T(8,128)(2,1)} %bitcast.28, s32[]{:T(128)S(6)} %select_n.59), kind=kLoop, calls=%fused_computation.18 | loop fusion | bytes 524292 | tf_op jit(solution)/shard_map/dynamic_slice | solution.py:83
  2.0 21.3 %collective-permute-start.3 = (bf16[1040,128]{1,0:T(8,128)(2,1)S(1)}, bf16[1040,128]{1,0:T(8,128)(2,1)S(1)}, u32[]{:S(2)}, u32[]{:S(2)}) collective-permute-start(bf16[1040,128]{1,0:T(8,128)(2,1)S(1)} %pad_maximum_fusion.3), channel_id=1, source_target_pairs={{960,0},{992,32},{128,64},{160,96},{64,128},{96,160},{256,192},{28... | collective-permute-start | bytes 798728 | tf_op jit(solution)/shard_map/ppermute | solution.py:88
  23.3 1.9 %collective-permute-start.2 = (bf16[1040,128]{1,0:T(8,128)(2,1)S(1)}, bf16[1040,128]{1,0:T(8,128)(2,1)S(1)}, u32[]{:S(2)}, u32[]{:S(2)}) collective-permute-start(bf16[1040,128]{1,0:T(8,128)(2,1)S(1)} %pad_maximum_fusion.3), channel_id=1, source_target_pairs={{992,0},{64,32},{32,64},{128,96},{96,128},{192,160},{160,192},{256... | collective-permute-start | bytes 798728 | tf_op jit(solution)/shard_map/ppermute | solution.py:88
  25.2 0.0 copy-done
  25.2 0.0 copy-start.1
  25.3 0.8 %pad_maximum_fusion.2 = bf16[2064,128]{1,0:T(8,128)(2,1)} fusion(bf16[16,128]{1,0:T(8,128)(2,1)S(1)} %scatter.4, bf16[2048,128]{1,0:T(8,128)(2,1)S(1)} %constant_dynamic-slice_fusion.1), kind=kLoop, calls=%fused_computation.2 | loop fusion | flops 1056768 | bytes 1056768 | tf_op jit(solution)/shard_map/concatenate | solution.py:83
  26.1 3.6 %collective-permute-start.1 = (bf16[2064,128]{1,0:T(8,128)(2,1)}, bf16[2064,128]{1,0:T(8,128)(2,1)S(1)}, u32[]{:S(2)}, u32[]{:S(2)}) collective-permute-start(bf16[2064,128]{1,0:T(8,128)(2,1)} %pad_maximum_fusion.2), channel_id=1, source_target_pairs={{64,0},{96,32},{0,64},{32,96},{192,128},{224,160},{128,192},{160,2... | collective-permute-start | bytes 1585160 | tf_op jit(solution)/shard_map/ppermute | solution.py:92
  29.7 1.9 %collective-permute-start = (bf16[2064,128]{1,0:T(8,128)(2,1)}, bf16[2064,128]{1,0:T(8,128)(2,1)S(1)}, u32[]{:S(2)}, u32[]{:S(2)}) collective-permute-start(bf16[2064,128]{1,0:T(8,128)(2,1)} %pad_maximum_fusion.2), channel_id=1, source_target_pairs={{32,0},{0,32},{96,64},{64,96},{160,128},{128,160},{224,192},{192,2... | collective-permute-start | bytes 1585160 | tf_op jit(solution)/shard_map/ppermute | solution.py:92
  31.6 0.0 copy-done.1
  31.7 15.7 %psum.7 = s32[8]{0:T(128)S(1)} all-reduce(s32[8]{0:T(128)S(1)} %get-tuple-element.29), channel_id=1, replica_groups=mesh['blk'=32,'col'=32] {'col'}, use_global_device_ids=true, to_apply=%region_0.0 | all-reduce | flops 8 | bytes 64 | tf_op jit(solution)/shard_map/psum | solution.py:101
  47.4 0.0 collective-permute-done.3.refs_8_
  47.4 0.0 collective-permute-done.2.refs_7_
  47.5 3.1 %collective-permute-start.4 = (bf16[1024,128]{1,0:T(8,128)(2,1)S(1)}, bf16[1024,128]{1,0:T(8,128)(2,1)S(1)}, u32[]{:S(2)}, u32[]{:S(2)}) collective-permute-start(bf16[1024,128]{1,0:T(8,128)(2,1)S(1)} %pad_maximum_fusion.4), channel_id=1, source_target_pairs={{28,0},{29,1},{30,2},{31,3},{0,4},{1,5},{2,6},{3,7},{4,8},{5,9},{6... | collective-permute-start | bytes 786440 | tf_op jit(solution)/shard_map/ppermute | solution.py:109
  50.6 3.4 %collective-permute-start.5 = (bf16[1024,128]{1,0:T(8,128)(2,1)S(1)}, bf16[1024,128]{1,0:T(8,128)(2,1)S(1)}, u32[]{:S(2)}, u32[]{:S(2)}) collective-permute-start(bf16[1024,128]{1,0:T(8,128)(2,1)S(1)} %pad_maximum_fusion.5), channel_id=1, source_target_pairs={{4,0},{5,1},{6,2},{7,3},{8,4},{9,5},{10,6},{11,7},{12,8},{13,9},{1... | collective-permute-start | bytes 786440 | tf_op jit(solution)/shard_map/ppermute | solution.py:110
  54.0 1.9 %collective-permute-done.4.refs_9_ = bf16[1024,128]{1,0:T(8,128)(2,1)S(1)} collective-permute-done((bf16[1024,128]{1,0:T(8,128)(2,1)S(1)}, bf16[1024,128]{1,0:T(8,128)(2,1)S(1)}, u32[]{:S(2)}, u32[]{:S(2)}) %collective-permute-start.4) | collective-permute-done | bytes 262176 | tf_op jit(solution)/shard_map/ppermute | solution.py:109
  56.0 0.0 collective-permute-done.1.refs_6_
  56.0 0.0 collective-permute-done.refs_5_
  56.0 1.1 %pad_maximum_fusion = bf16[4128,128]{1,0:T(8,128)(2,1)} fusion(bf16[2064,128]{1,0:T(8,128)(2,1)S(1)} %collective-permute-done.1.refs_6_, bf16[2064,128]{1,0:T(8,128)(2,1)S(1)} %collective-permute-done.refs_5_), kind=kLoop, calls=%fused_computation | loop fusion | flops 2113536 | bytes 2113536 | tf_op jit(solution)/shard_map/concatenate | solution.py:105
  57.0 1.0 %collective-permute-done.5.refs_10_ = bf16[1024,128]{1,0:T(8,128)(2,1)S(1)} collective-permute-done((bf16[1024,128]{1,0:T(8,128)(2,1)S(1)}, bf16[1024,128]{1,0:T(8,128)(2,1)S(1)}, u32[]{:S(2)}, u32[]{:S(2)}) %collective-permute-start.5) | collective-permute-done | bytes 262176 | tf_op jit(solution)/shard_map/ppermute | solution.py:110
  58.0 6.1 %collective-permute-start.6 = (bf16[4128,128]{1,0:T(8,128)(2,1)}, bf16[4128,128]{1,0:T(8,128)(2,1)}, u32[]{:S(2)}, u32[]{:S(2)}) collective-permute-start(bf16[4128,128]{1,0:T(8,128)(2,1)} %pad_maximum_fusion), channel_id=1, source_target_pairs={{1,0},{0,1},{3,2},{2,3},{5,4},{4,5},{7,6},{6,7},{9,8},{8,9},{11,10... | collective-permute-start | bytes 3170312 | tf_op jit(solution)/shard_map/ppermute | solution.py:105
  64.1 1.1 %pad_maximum_fusion.1 = bf16[4128,128]{1,0:T(8,128)(2,1)} fusion(bf16[1040,128]{1,0:T(8,128)(2,1)S(1)} %collective-permute-done.3.refs_8_, bf16[1040,128]{1,0:T(8,128)(2,1)S(1)} %collective-permute-done.2.refs_7_, bf16[1024,128]{1,0:T(8,128)(2,1)S(1)} %collective-permute-done.5.refs_10_, bf16[1024,128]{1,0:T(8,128)(2,1)S(1)} %collective-permute-done.4.refs_9_), kind=kLoop, calls=%fused_computation.1 | loop fusion | flops 4227072 | bytes 2113536 | tf_op jit(solution)/shard_map/concatenate | solution.py:105
  65.2 1.9 %collective-permute-start.7 = (bf16[4128,128]{1,0:T(8,128)(2,1)}, bf16[4128,128]{1,0:T(8,128)(2,1)}, u32[]{:S(2)}, u32[]{:S(2)}) collective-permute-start(bf16[4128,128]{1,0:T(8,128)(2,1)} %pad_maximum_fusion.1), channel_id=1, source_target_pairs={{1,0},{0,1},{3,2},{2,3},{5,4},{4,5},{7,6},{6,7},{9,8},{8,9},{11,10... | collective-permute-start | bytes 3170312 | tf_op jit(solution)/shard_map/ppermute | solution.py:105
  67.2 0.1 convert_element_type.20
  67.3 0.1 stack.67.refs_0_
  67.4 0.1 concatenate.27
  67.5 0.0 collective-permute-done.6.refs_11_
  67.5 2.6 %collective-permute-done.7.refs_12_ = bf16[4128,128]{1,0:T(8,128)(2,1)} collective-permute-done((bf16[4128,128]{1,0:T(8,128)(2,1)}, bf16[4128,128]{1,0:T(8,128)(2,1)}, u32[]{:S(2)}, u32[]{:S(2)}) %collective-permute-start.7) | collective-permute-done | bytes 1056800 | tf_op jit(solution)/shard_map/ppermute | solution.py:105
  70.1 5.4 %purify.1 = bf16[8,1,128,128]{3,2,1,0:T(8,128)(2,1)} custom-call(s32[17]{0:T(128)S(1)} %stack.67.refs_0_, s32[160]{0:T(256)S(1)} %subtract_and_fusion.refs_1_, s32[8]{0:T(128)S(1)} %get-tuple-element.30.refs_2_, s32[8]{0:T(128)S(1)} %iota_add_fusion.refs_3_, bf16[4096,128]{1,0:T(8,128)(2,1)S(1)} %bitcast.30, ...), custom_call_target="tpu_custom_call" | custom-call | tf_op jit(solution)/shard_map/purify/pallas_call | solution.py:150
  (11 shorter events, 0.2 us)
Async XLA Ops:
  0.0 25.2 %copy-start = (bf16[8,4,128,128]{3,2,1,0:T(8,128)(2,1)S(1)}, bf16[8,4,128,128]{3,2,1,0:T(8,128)(2,1)}, u32[]{:S(2)}) copy-start(bf16[8,4,128,128]{3,2,1,0:T(8,128)(2,1)} %param.5) | copy-start | bytes 3145732
  2.0 45.4 %collective-permute-start.3 = (bf16[1040,128]{1,0:T(8,128)(2,1)S(1)}, bf16[1040,128]{1,0:T(8,128)(2,1)S(1)}, u32[]{:S(2)}, u32[]{:S(2)}) collective-permute-start(bf16[1040,128]{1,0:T(8,128)(2,1)S(1)} %pad_maximum_fusion.3), channel_id=1, source_target_pairs={{960,0},{992,32},{128,64},{160,96},{64,128},{96,160},{256,192},{28... | collective-permute-start | bytes 798728 | tf_op jit(solution)/shard_map/ppermute | solution.py:88
  23.3 24.1 %collective-permute-start.2 = (bf16[1040,128]{1,0:T(8,128)(2,1)S(1)}, bf16[1040,128]{1,0:T(8,128)(2,1)S(1)}, u32[]{:S(2)}, u32[]{:S(2)}) collective-permute-start(bf16[1040,128]{1,0:T(8,128)(2,1)S(1)} %pad_maximum_fusion.3), channel_id=1, source_target_pairs={{992,0},{64,32},{32,64},{128,96},{96,128},{192,160},{160,192},{256... | collective-permute-start | bytes 798728 | tf_op jit(solution)/shard_map/ppermute | solution.py:88
  25.2 6.4 %copy-start.1 = (s32[8,1]{0,1:T(1,128)S(1)}, s32[8,1]{0,1:T(1,128)}, u32[]{:S(2)}) copy-start(s32[8,1]{0,1:T(1,128)} %param.7) | copy-start | bytes 100
  26.1 29.8 %collective-permute-start.1 = (bf16[2064,128]{1,0:T(8,128)(2,1)}, bf16[2064,128]{1,0:T(8,128)(2,1)S(1)}, u32[]{:S(2)}, u32[]{:S(2)}) collective-permute-start(bf16[2064,128]{1,0:T(8,128)(2,1)} %pad_maximum_fusion.2), channel_id=1, source_target_pairs={{64,0},{96,32},{0,64},{32,96},{192,128},{224,160},{128,192},{160,2... | collective-permute-start | bytes 1585160 | tf_op jit(solution)/shard_map/ppermute | solution.py:92
  29.7 26.3 %collective-permute-start = (bf16[2064,128]{1,0:T(8,128)(2,1)}, bf16[2064,128]{1,0:T(8,128)(2,1)S(1)}, u32[]{:S(2)}, u32[]{:S(2)}) collective-permute-start(bf16[2064,128]{1,0:T(8,128)(2,1)} %pad_maximum_fusion.2), channel_id=1, source_target_pairs={{32,0},{0,32},{96,64},{64,96},{160,128},{128,160},{224,192},{192,2... | collective-permute-start | bytes 1585160 | tf_op jit(solution)/shard_map/ppermute | solution.py:92
  47.5 8.5 %collective-permute-start.4 = (bf16[1024,128]{1,0:T(8,128)(2,1)S(1)}, bf16[1024,128]{1,0:T(8,128)(2,1)S(1)}, u32[]{:S(2)}, u32[]{:S(2)}) collective-permute-start(bf16[1024,128]{1,0:T(8,128)(2,1)S(1)} %pad_maximum_fusion.4), channel_id=1, source_target_pairs={{28,0},{29,1},{30,2},{31,3},{0,4},{1,5},{2,6},{3,7},{4,8},{5,9},{6... | collective-permute-start | bytes 786440 | tf_op jit(solution)/shard_map/ppermute | solution.py:109
  50.6 7.4 %collective-permute-start.5 = (bf16[1024,128]{1,0:T(8,128)(2,1)S(1)}, bf16[1024,128]{1,0:T(8,128)(2,1)S(1)}, u32[]{:S(2)}, u32[]{:S(2)}) collective-permute-start(bf16[1024,128]{1,0:T(8,128)(2,1)S(1)} %pad_maximum_fusion.5), channel_id=1, source_target_pairs={{4,0},{5,1},{6,2},{7,3},{8,4},{9,5},{10,6},{11,7},{12,8},{13,9},{1... | collective-permute-start | bytes 786440 | tf_op jit(solution)/shard_map/ppermute | solution.py:110
  58.0 9.5 %collective-permute-start.6 = (bf16[4128,128]{1,0:T(8,128)(2,1)}, bf16[4128,128]{1,0:T(8,128)(2,1)}, u32[]{:S(2)}, u32[]{:S(2)}) collective-permute-start(bf16[4128,128]{1,0:T(8,128)(2,1)} %pad_maximum_fusion), channel_id=1, source_target_pairs={{1,0},{0,1},{3,2},{2,3},{5,4},{4,5},{7,6},{6,7},{9,8},{8,9},{11,10... | collective-permute-start | bytes 3170312 | tf_op jit(solution)/shard_map/ppermute | solution.py:105
  65.2 4.9 %collective-permute-start.7 = (bf16[4128,128]{1,0:T(8,128)(2,1)}, bf16[4128,128]{1,0:T(8,128)(2,1)}, u32[]{:S(2)}, u32[]{:S(2)}) collective-permute-start(bf16[4128,128]{1,0:T(8,128)(2,1)} %pad_maximum_fusion.1), channel_id=1, source_target_pairs={{1,0},{0,1},{3,2},{2,3},{5,4},{4,5},{7,6},{6,7},{9,8},{8,9},{11,10... | collective-permute-start | bytes 3170312 | tf_op jit(solution)/shard_map/ppermute | solution.py:105

commit v6 on v4

--- a/solution.py
+++ b/solution.py
@@ -104,13 +104,14 @@
     def from_core(arrays):
         return lax.ppermute(jnp.concatenate(arrays, 0), "col", col_routes(lambda i: i ^ 1))
 
-    first = jnp.concatenate([x[:eighth] for x in late], 0)
-    second = jnp.concatenate([x[eighth:quarter] for x in late], 0)
-    (first, second), early = lax.optimization_barrier(((first, second), early))
-    left = lax.ppermute(first, "col", col_routes(lambda i: i - 4))
-    right = lax.ppermute(second, "col", col_routes(lambda i: i + 4))
-    other = from_core(early)
-    sides = from_core([left, right, *late])
+    left = lax.ppermute(
+        jnp.concatenate([x[:eighth] for x in late], 0), "col", col_routes(lambda i: i - 4)
+    )
+    right = lax.ppermute(
+        jnp.concatenate([x[eighth:quarter] for x in late], 0), "col", col_routes(lambda i: i + 4)
+    )
+    others = [from_core(early), from_core(late)]
+    sides = from_core([left, right])
 
     def listed(x):
         return x[x.shape[0] - 16, : own_cols.shape[0]]
@@ -122,7 +123,7 @@
         [behind[1], behind[0], own_cols.astype(jnp.bfloat16), ahead[0], ahead[1]]
     )
     window_cols = local(window_cols.astype(jnp.int32))
-    pieces = [flat, *early, *late, left, right, other, sides]
+    pieces = [flat, *early, *late, left, right, *others, sides]
     near, far = (
         [(REACH + jnp.where(o, -way, way) * d) * panel for o, d in zip(odd, (1, 2))]
         for way in (1, -1)
@@ -136,12 +137,10 @@
     for shift in (0, eighth):
         layout.append([(0, eighth), (eighth, eighth)])
         targets += [top + site[1, 0] + shift for top in far]
-    layout.append([(0, half), (half + 16, half)])
-    targets += [top + (1 - core) * half for top in near]
+    layout += [[(0, rows), (rows + 16, rows)] for rows in (half, quarter)]
+    targets += [top + (1 - core) * half for top in near] + [top + site[0, 1] for top in far]
     layout.append([(j * eighth, eighth) for j in range(4)])
-    layout[-1] += [(2 * quarter + j * (quarter + 16), quarter) for j in range(2)]
     targets += [top + site[1, 1] + shift for shift in (0, eighth) for top in far]
-    targets += [top + site[0, 1] for top in far]
     targets = jnp.stack(targets).astype(jnp.int32)
 
     smem = pl.BlockSpec(memory_space=pltpu.SMEM)

time: 81.7 us -> 74.5 us (0.912)
  the two profiles are of different devices: /device:TPU:7 before, /device:TPU:1 now
where the time goes in v6:
time: 74.5 us; the launch traced here: 74.1 us
  starting transfers between devices  44.6 us (60%)
  blocking collectives  15.8 us (21%)
  Pallas kernels  5.39 us (7%)
  other arithmetic  4.48 us (6%)
  waiting for transfers between devices  2.05 us (3%)
  local copies, waits for them, and re-layouts  1.55 us (2%)
    ppermute x2, starting transfers between devices, body(): lax.ppermute(small, 'blk', swap_routes(lambda i, d=d: ((i + d ^ d) - d) %...  24.2 us
    psum x1, blocking collectives, body(): late, skipped = lax.optimization_barrier((late, lax.psum(offsets, 'col')))  15.8 us
    ppermute x3, starting transfers between devices, from_core(): lax.ppermute(jnp.concatenate(arrays, 0), 'col', col_routes(lambda i: i ^ 1))  10.1 us
    pallas_call x1, Pallas kernels, body(): pl.pallas_call(lambda *refs: purify_kernel(layout, bs, slots, *refs), out...  5.39 us
    ppermute x2, starting transfers between devices, body(): lax.ppermute(large, 'blk', swap_routes(lambda i, d=d: i ^ d))  3.83 us
    ppermute x1, starting transfers between devices, body(): lax.ppermute(jnp.concatenate([x[eighth:quarter] for x in late], 0), 'col'...  3.37 us
    ppermute x1, starting transfers between devices, body(): lax.ppermute(jnp.concatenate([x[:eighth] for x in late], 0), 'col', col_r...  3.12 us
    concatenate x3, other arithmetic, from_core(): jnp.concatenate(arrays, 0)  2.77 us
  transfers between devices with their start and end apart: 9, of which 2 were waited for; matrix products, arithmetic and copies ran while one was open for 5% of the time, Pallas kernels for 0%

profile of v6, /device:TPU:1, one launch (start us, length us, event | category | flops | bytes accessed | tf_op | source)
XLA Modules:
  0.0 74.1 jit_solution(2507859109938223562)
XLA Ops:
  0.0 0.0 copy-start
  0.0 0.8 %convert_element_type.18 = bf16[8,4]{0,1:T(4,128)(2,1)S(1)} convert(s32[8,4]{0,1:T(4,128)} %param.6) | non-fusion elementwise | flops 32 | bytes 192 | tf_op jit(solution)/shard_map/convert_element_type | solution.py:80
  0.8 0.1 copy.6
  0.9 0.1 convert_element_type.19
  1.0 1.0 %constant_dynamic-slice_fusion = bf16[1024,128]{1,0:T(8,128)(2,1)S(1)} fusion(bf16[4096,128]{1,0:T(8,128)(2,1)} %bitcast.28, s32[]{:T(128)S(6)} %select_n.59), kind=kLoop, calls=%fused_computation.19 | loop fusion | bytes 524292 | tf_op jit(solution)/shard_map/dynamic_slice | solution.py:83
  2.0 20.6 %collective-permute-start.1 = (bf16[1040,128]{1,0:T(8,128)(2,1)S(1)}, bf16[1040,128]{1,0:T(8,128)(2,1)S(1)}, u32[]{:S(2)}, u32[]{:S(2)}) collective-permute-start(bf16[1040,128]{1,0:T(8,128)(2,1)S(1)} %pad_maximum_fusion.4), channel_id=1, source_target_pairs={{992,0},{64,32},{32,64},{128,96},{96,128},{192,160},{160,192},{256... | collective-permute-start | bytes 798728 | tf_op jit(solution)/shard_map/ppermute | solution.py:88
  22.6 3.5 %collective-permute-start.2 = (bf16[1040,128]{1,0:T(8,128)(2,1)S(1)}, bf16[1040,128]{1,0:T(8,128)(2,1)S(1)}, u32[]{:S(2)}, u32[]{:S(2)}) collective-permute-start(bf16[1040,128]{1,0:T(8,128)(2,1)S(1)} %pad_maximum_fusion.4), channel_id=1, source_target_pairs={{960,0},{992,32},{128,64},{160,96},{64,128},{96,160},{256,192},{28... | collective-permute-start | bytes 798728 | tf_op jit(solution)/shard_map/ppermute | solution.py:88
  26.2 0.0 copy-done
  26.2 0.0 copy-start.1
  26.2 0.8 %pad_maximum_fusion.2 = bf16[2064,128]{1,0:T(8,128)(2,1)} fusion(bf16[16,128]{1,0:T(8,128)(2,1)S(1)} %scatter.4, bf16[2048,128]{1,0:T(8,128)(2,1)S(1)} %constant_dynamic-slice_fusion.1), kind=kLoop, calls=%fused_computation.2 | loop fusion | flops 1056768 | bytes 1056768 | tf_op jit(solution)/shard_map/concatenate | solution.py:83
  27.1 1.9 %collective-permute-start = (bf16[2064,128]{1,0:T(8,128)(2,1)}, bf16[2064,128]{1,0:T(8,128)(2,1)S(1)}, u32[]{:S(2)}, u32[]{:S(2)}) collective-permute-start(bf16[2064,128]{1,0:T(8,128)(2,1)} %pad_maximum_fusion.2), channel_id=1, source_target_pairs={{64,0},{96,32},{0,64},{32,96},{192,128},{224,160},{128,192},{160,2... | collective-permute-start | bytes 1585160 | tf_op jit(solution)/shard_map/ppermute | solution.py:92
  29.0 1.9 %collective-permute-start.3 = (bf16[2064,128]{1,0:T(8,128)(2,1)}, bf16[2064,128]{1,0:T(8,128)(2,1)S(1)}, u32[]{:S(2)}, u32[]{:S(2)}) collective-permute-start(bf16[2064,128]{1,0:T(8,128)(2,1)} %pad_maximum_fusion.2), channel_id=1, source_target_pairs={{32,0},{0,32},{96,64},{64,96},{160,128},{128,160},{224,192},{192,2... | collective-permute-start | bytes 1585160 | tf_op jit(solution)/shard_map/ppermute | solution.py:92
  30.9 0.0 copy-done.1
  31.0 15.8 %psum.7 = s32[8]{0:T(128)S(1)} all-reduce(s32[8]{0:T(128)S(1)} %get-tuple-element.23), channel_id=1, replica_groups=mesh['blk'=32,'col'=32] {'col'}, use_global_device_ids=true, to_apply=%region_0.0 | all-reduce | flops 8 | bytes 64 | tf_op jit(solution)/shard_map/psum | solution.py:101
  46.7 0.1 convert_element_type.20
  46.8 0.1 stack.67.refs_0_
  46.9 0.0 collective-permute-done.1.refs_7_
  46.9 0.3 collective-permute-done.2.refs_8_
  47.2 0.1 fusion.4
  47.3 3.1 %collective-permute-start.4 = (bf16[1024,128]{1,0:T(8,128)(2,1)S(1)}, bf16[1024,128]{1,0:T(8,128)(2,1)S(1)}, u32[]{:S(2)}, u32[]{:S(2)}) collective-permute-start(bf16[1024,128]{1,0:T(8,128)(2,1)S(1)} %pad_maximum_fusion.5), channel_id=1, source_target_pairs={{28,0},{29,1},{30,2},{31,3},{0,4},{1,5},{2,6},{3,7},{4,8},{5,9},{6... | collective-permute-start | bytes 786440 | tf_op jit(solution)/shard_map/ppermute | solution.py:107
  50.5 3.4 %collective-permute-start.5 = (bf16[1024,128]{1,0:T(8,128)(2,1)S(1)}, bf16[1024,128]{1,0:T(8,128)(2,1)S(1)}, u32[]{:S(2)}, u32[]{:S(2)}) collective-permute-start(bf16[1024,128]{1,0:T(8,128)(2,1)S(1)} %pad_maximum_fusion.6), channel_id=1, source_target_pairs={{4,0},{5,1},{6,2},{7,3},{8,4},{9,5},{10,6},{11,7},{12,8},{13,9},{1... | collective-permute-start | bytes 786440 | tf_op jit(solution)/shard_map/ppermute | solution.py:110
  53.8 0.8 %pad_maximum_fusion.1 = bf16[2080,128]{1,0:T(8,128)(2,1)} fusion(bf16[1040,128]{1,0:T(8,128)(2,1)S(1)} %collective-permute-done.2.refs_8_, bf16[1040,128]{1,0:T(8,128)(2,1)S(1)} %collective-permute-done.1.refs_7_), kind=kLoop, calls=%fused_computation.1 | loop fusion | flops 1064960 | bytes 1064960 | tf_op jit(solution)/shard_map/concatenate | solution.py:105
  54.7 5.8 %collective-permute-start.7 = (bf16[2080,128]{1,0:T(8,128)(2,1)}, bf16[2080,128]{1,0:T(8,128)(2,1)}, u32[]{:S(2)}, u32[]{:S(2)}) collective-permute-start(bf16[2080,128]{1,0:T(8,128)(2,1)} %pad_maximum_fusion.1), channel_id=1, source_target_pairs={{1,0},{0,1},{3,2},{2,3},{5,4},{4,5},{7,6},{6,7},{9,8},{8,9},{11,10... | collective-permute-start | bytes 1597448 | tf_op jit(solution)/shard_map/ppermute | solution.py:105
  60.5 0.0 collective-permute-done.refs_6_
  60.5 0.0 collective-permute-done.3.refs_5_
  60.6 1.1 %pad_maximum_fusion = bf16[4128,128]{1,0:T(8,128)(2,1)} fusion(bf16[2064,128]{1,0:T(8,128)(2,1)S(1)} %collective-permute-done.refs_6_, bf16[2064,128]{1,0:T(8,128)(2,1)S(1)} %collective-permute-done.3.refs_5_), kind=kLoop, calls=%fused_computation | loop fusion | flops 2113536 | bytes 2113536 | tf_op jit(solution)/shard_map/concatenate | solution.py:105
  61.6 1.9 %collective-permute-start.6 = (bf16[4128,128]{1,0:T(8,128)(2,1)}, bf16[4128,128]{1,0:T(8,128)(2,1)}, u32[]{:S(2)}, u32[]{:S(2)}) collective-permute-start(bf16[4128,128]{1,0:T(8,128)(2,1)} %pad_maximum_fusion), channel_id=1, source_target_pairs={{1,0},{0,1},{3,2},{2,3},{5,4},{4,5},{7,6},{6,7},{9,8},{8,9},{11,10... | collective-permute-start | bytes 3170312 | tf_op jit(solution)/shard_map/ppermute | solution.py:105
  63.6 0.0 collective-permute-done.4.refs_9_
  63.6 0.0 collective-permute-done.5.refs_10_
  63.6 0.8 %pad_maximum_fusion.3 = bf16[2048,128]{1,0:T(8,128)(2,1)} fusion(bf16[1024,128]{1,0:T(8,128)(2,1)S(1)} %collective-permute-done.5.refs_10_, bf16[1024,128]{1,0:T(8,128)(2,1)S(1)} %collective-permute-done.4.refs_9_), kind=kLoop, calls=%fused_computation.3 | loop fusion | flops 1048576 | bytes 1048576 | tf_op jit(solution)/shard_map/concatenate | solution.py:105
  64.4 2.4 %collective-permute-start.8 = (bf16[2048,128]{1,0:T(8,128)(2,1)}, bf16[2048,128]{1,0:T(8,128)(2,1)}, u32[]{:S(2)}, u32[]{:S(2)}) collective-permute-start(bf16[2048,128]{1,0:T(8,128)(2,1)} %pad_maximum_fusion.3), channel_id=1, source_target_pairs={{1,0},{0,1},{3,2},{2,3},{5,4},{4,5},{7,6},{6,7},{9,8},{8,9},{11,10... | collective-permute-start | bytes 1572872 | tf_op jit(solution)/shard_map/ppermute | solution.py:105
  66.9 0.1 concatenate.28
  67.0 0.0 collective-permute-done.7.refs_12_
  67.0 1.7 %collective-permute-done.8.refs_13_ = bf16[2048,128]{1,0:T(8,128)(2,1)} collective-permute-done((bf16[2048,128]{1,0:T(8,128)(2,1)}, bf16[2048,128]{1,0:T(8,128)(2,1)}, u32[]{:S(2)}, u32[]{:S(2)}) %collective-permute-start.8) | collective-permute-done | bytes 524320 | tf_op jit(solution)/shard_map/ppermute | solution.py:105
  68.7 0.0 collective-permute-done.6.refs_11_
  68.7 5.4 %purify.1 = bf16[8,1,128,128]{3,2,1,0:T(8,128)(2,1)} custom-call(s32[17]{0:T(128)S(1)} %stack.67.refs_0_, s32[160]{0:T(256)S(1)} %subtract_and_fusion.refs_1_, s32[8]{0:T(128)S(1)} %get-tuple-element.24.refs_2_, s32[8]{0:T(128)S(1)} %iota_add_fusion.refs_3_, bf16[4096,128]{1,0:T(8,128)(2,1)S(1)} %bitcast.30, ...), custom_call_target="tpu_custom_call" | custom-call | tf_op jit(solution)/shard_map/purify/pallas_call | solution.py:148
  (10 shorter events, 0.1 us)
Async XLA Ops:
  0.0 26.2 %copy-start = (bf16[8,4,128,128]{3,2,1,0:T(8,128)(2,1)S(1)}, bf16[8,4,128,128]{3,2,1,0:T(8,128)(2,1)}, u32[]{:S(2)}) copy-start(bf16[8,4,128,128]{3,2,1,0:T(8,128)(2,1)} %param.5) | copy-start | bytes 3145732
  2.0 44.9 %collective-permute-start.1 = (bf16[1040,128]{1,0:T(8,128)(2,1)S(1)}, bf16[1040,128]{1,0:T(8,128)(2,1)S(1)}, u32[]{:S(2)}, u32[]{:S(2)}) collective-permute-start(bf16[1040,128]{1,0:T(8,128)(2,1)S(1)} %pad_maximum_fusion.4), channel_id=1, source_target_pairs={{992,0},{64,32},{32,64},{128,96},{96,128},{192,160},{160,192},{256... | collective-permute-start | bytes 798728 | tf_op jit(solution)/shard_map/ppermute | solution.py:88
  22.6 24.6 %collective-permute-start.2 = (bf16[1040,128]{1,0:T(8,128)(2,1)S(1)}, bf16[1040,128]{1,0:T(8,128)(2,1)S(1)}, u32[]{:S(2)}, u32[]{:S(2)}) collective-permute-start(bf16[1040,128]{1,0:T(8,128)(2,1)S(1)} %pad_maximum_fusion.4), channel_id=1, source_target_pairs={{960,0},{992,32},{128,64},{160,96},{64,128},{96,160},{256,192},{28... | collective-permute-start | bytes 798728 | tf_op jit(solution)/shard_map/ppermute | solution.py:88
  26.2 4.8 %copy-start.1 = (s32[8,1]{0,1:T(1,128)S(1)}, s32[8,1]{0,1:T(1,128)}, u32[]{:S(2)}) copy-start(s32[8,1]{0,1:T(1,128)} %param.7) | copy-start | bytes 100
  27.1 33.4 %collective-permute-start = (bf16[2064,128]{1,0:T(8,128)(2,1)}, bf16[2064,128]{1,0:T(8,128)(2,1)S(1)}, u32[]{:S(2)}, u32[]{:S(2)}) collective-permute-start(bf16[2064,128]{1,0:T(8,128)(2,1)} %pad_maximum_fusion.2), channel_id=1, source_target_pairs={{64,0},{96,32},{0,64},{32,96},{192,128},{224,160},{128,192},{160,2... | collective-permute-start | bytes 1585160 | tf_op jit(solution)/shard_map/ppermute | solution.py:92
  29.0 31.5 %collective-permute-start.3 = (bf16[2064,128]{1,0:T(8,128)(2,1)}, bf16[2064,128]{1,0:T(8,128)(2,1)S(1)}, u32[]{:S(2)}, u32[]{:S(2)}) collective-permute-start(bf16[2064,128]{1,0:T(8,128)(2,1)} %pad_maximum_fusion.2), channel_id=1, source_target_pairs={{32,0},{0,32},{96,64},{64,96},{160,128},{128,160},{224,192},{192,2... | collective-permute-start | bytes 1585160 | tf_op jit(solution)/shard_map/ppermute | solution.py:92
  47.3 16.2 %collective-permute-start.4 = (bf16[1024,128]{1,0:T(8,128)(2,1)S(1)}, bf16[1024,128]{1,0:T(8,128)(2,1)S(1)}, u32[]{:S(2)}, u32[]{:S(2)}) collective-permute-start(bf16[1024,128]{1,0:T(8,128)(2,1)S(1)} %pad_maximum_fusion.5), channel_id=1, source_target_pairs={{28,0},{29,1},{30,2},{31,3},{0,4},{1,5},{2,6},{3,7},{4,8},{5,9},{6... | collective-permute-start | bytes 786440 | tf_op jit(solution)/shard_map/ppermute | solution.py:107
  50.5 13.1 %collective-permute-start.5 = (bf16[1024,128]{1,0:T(8,128)(2,1)S(1)}, bf16[1024,128]{1,0:T(8,128)(2,1)S(1)}, u32[]{:S(2)}, u32[]{:S(2)}) collective-permute-start(bf16[1024,128]{1,0:T(8,128)(2,1)S(1)} %pad_maximum_fusion.6), channel_id=1, source_target_pairs={{4,0},{5,1},{6,2},{7,3},{8,4},{9,5},{10,6},{11,7},{12,8},{13,9},{1... | collective-permute-start | bytes 786440 | tf_op jit(solution)/shard_map/ppermute | solution.py:110
  54.7 12.3 %collective-permute-start.7 = (bf16[2080,128]{1,0:T(8,128)(2,1)}, bf16[2080,128]{1,0:T(8,128)(2,1)}, u32[]{:S(2)}, u32[]{:S(2)}) collective-permute-start(bf16[2080,128]{1,0:T(8,128)(2,1)} %pad_maximum_fusion.1), channel_id=1, source_target_pairs={{1,0},{0,1},{3,2},{2,3},{5,4},{4,5},{7,6},{6,7},{9,8},{8,9},{11,10... | collective-permute-start | bytes 1597448 | tf_op jit(solution)/shard_map/ppermute | solution.py:105
  61.6 7.1 %collective-permute-start.6 = (bf16[4128,128]{1,0:T(8,128)(2,1)}, bf16[4128,128]{1,0:T(8,128)(2,1)}, u32[]{:S(2)}, u32[]{:S(2)}) collective-permute-start(bf16[4128,128]{1,0:T(8,128)(2,1)} %pad_maximum_fusion), channel_id=1, source_target_pairs={{1,0},{0,1},{3,2},{2,3},{5,4},{4,5},{7,6},{6,7},{9,8},{8,9},{11,10... | collective-permute-start | bytes 3170312 | tf_op jit(solution)/shard_map/ppermute | solution.py:105
  64.4 4.3 %collective-permute-start.8 = (bf16[2048,128]{1,0:T(8,128)(2,1)}, bf16[2048,128]{1,0:T(8,128)(2,1)}, u32[]{:S(2)}, u32[]{:S(2)}) collective-permute-start(bf16[2048,128]{1,0:T(8,128)(2,1)} %pad_maximum_fusion.3), channel_id=1, source_target_pairs={{1,0},{0,1},{3,2},{2,3},{5,4},{4,5},{7,6},{6,7},{9,8},{8,9},{11,10... | collective-permute-start | bytes 1572872 | tf_op jit(solution)/shard_map/ppermute | solution.py:105
